TPU v7x, 512 devices: a whole 4x8x8 slice. The times are simulated.
512 devices in a mesh: row: 16 (over y_lo, x), col: 32 (over z, y_hi, core).
Axes of the slice: x: 4, y: 8 (y_hi: 2, y_lo: 4; y = y_hi * 4 + y_lo), z: 8, core: 2. Of those that a mesh axis runs over, the one named last changes fastest.
Arguments:
- features: bfloat16 [65536, 1024], P(('row', 'col')), may hold values from -24 to 24
- degree: int32 [65536], P(('row', 'col')), may hold values from 16 to 128
- blocks: bfloat16 [16, 32, 72, 128, 128], P('row', 'col'), may hold values from 0 to 1
- coords: int32 [16, 32, 72], P('row', 'col'), may hold values from 0 to 511, as said below
- counts: int32 [16, 32], P('row', 'col'), may hold values from 18 to 72, as said below
- w_self: bfloat16 [1024, 256], replicated, may hold values from -0.1875 to 0.1875
- w_neigh: bfloat16 [1024, 256], replicated, may hold values from -0.1875 to 0.1875
- offset: bfloat16 [256], replicated, may hold values from -3 to 3
- cotangent: bfloat16 [65536, 256], P(('row', 'col')), may hold values from -6 to 6
Outputs:
- node_out: bfloat16 [65536, 256], P(('row', 'col'))
- feat_grad: bfloat16 [65536, 1024], P(('row', 'col'))
- self_grad: bfloat16 [1024, 256], replicated
- neigh_grad: bfloat16 [1024, 256], replicated
- offset_grad: float32 [256], replicated
Inputs may be any that keep to these rules, and one draw needn't show every extreme that they name: `coords`: within each entry (a, b) all 72 coordinates differ; each is i * 16 + j with i < 32 and j < 16. `counts`: some device uses all 72 slots in every draw.
All inputs are finite; a program needn't handle non-finite values.
Results may differ from a plain program's by a relative error of at most 0.022.
Values may be sent and summed in bfloat16 or wider, within the bound.
A program may use at most 64 MiB of HBM per device.

v0:
```python
import math

import jax
import jax.numpy as jnp
from jax import lax
from jax.sharding import PartitionSpec as P


def body(features, degree, blocks, coords, counts, w_self, w_neigh, offset, cotangent):
    nodes_dev, hidden = cotangent.shape
    slot_count = blocks.shape[2]
    block_size = blocks.shape[3]
    row_grid = lax.axis_size("row")
    col_grid = lax.axis_size("col")
    src_count = row_grid * nodes_dev // block_size
    dest_count = col_grid * nodes_dev // block_size
    tiles = blocks[0, 0]
    codes = coords[0, 0]
    filled = lax.iota(jnp.int32, slot_count) < counts[0, 0]
    dest_idx = codes // src_count
    src_idx = codes % src_count
    dest_target = jnp.where(filled, dest_idx, dest_count)
    src_target = jnp.where(filled, src_idx, src_count)
    projected = jnp.dot(features, w_neigh, preferred_element_type=jnp.float32).astype(jnp.bfloat16)
    row_panel = lax.all_gather(projected, "row", axis=0, tiled=True)
    picked = row_panel.reshape(src_count, block_size, hidden)[src_idx]
    products = jnp.einsum("kij,kjh->kih", tiles, picked, preferred_element_type=jnp.float32)
    partial_value = jax.ops.segment_sum(products, dest_target, num_segments=dest_count + 1)[
        :dest_count
    ]
    partial_value = partial_value.reshape(dest_count * block_size, hidden)
    aggregate = lax.psum_scatter(
        partial_value.astype(jnp.bfloat16), "col", scatter_dimension=0, tiled=True
    ).astype(jnp.float32)
    degree_f = degree.astype(jnp.float32)[:, None]
    preact = (
        jnp.dot(features, w_self, preferred_element_type=jnp.float32)
        + aggregate / degree_f
        + offset.astype(jnp.float32)[None, :]
    )
    sigmoid_pre = jax.nn.sigmoid(preact)
    node_out = (preact * sigmoid_pre).astype(jnp.bfloat16)
    dpre = cotangent.astype(jnp.float32) * sigmoid_pre * (1.0 + preact * (1.0 - sigmoid_pre))
    dpre_b = dpre.astype(jnp.bfloat16)
    dscaled = (dpre / degree_f).astype(jnp.bfloat16)
    dest_rows = lax.all_gather(dscaled, "col", axis=0, tiled=True)
    chosen = dest_rows.reshape(dest_count, block_size, hidden)[dest_idx]
    reversed_products = jnp.einsum(
        "kij,kih->kjh", tiles, chosen, preferred_element_type=jnp.float32
    )
    returned = jax.ops.segment_sum(reversed_products, src_target, num_segments=src_count + 1)[
        :src_count
    ]
    returned = returned.reshape(src_count * block_size, hidden)
    summed = lax.psum(returned.astype(jnp.bfloat16), "row").astype(jnp.float32)
    dprop = lax.dynamic_slice_in_dim(summed, lax.axis_index("row") * nodes_dev, nodes_dev, 0)
    dprop_b = dprop.astype(jnp.bfloat16)
    feat_grad = (
        jnp.einsum("nh,fh->nf", dpre_b, w_self, preferred_element_type=jnp.float32)
        + jnp.einsum("nh,fh->nf", dprop_b, w_neigh, preferred_element_type=jnp.float32)
    ).astype(jnp.bfloat16)
    self_term = jnp.einsum("nf,nh->fh", features, dpre_b, preferred_element_type=jnp.float32)
    neigh_term = jnp.einsum("nf,nh->fh", features, dprop_b, preferred_element_type=jnp.float32)
    offset_term = jnp.sum(dpre, axis=0)
    self_sum, neigh_sum, offset_sum = lax.psum((self_term, neigh_term, offset_term), ("row", "col"))
    grad_scale = 1.0 / math.sqrt(nodes_dev * row_grid * col_grid)
    self_grad = (self_sum * grad_scale).astype(jnp.bfloat16)
    neigh_grad = (neigh_sum * grad_scale).astype(jnp.bfloat16)
    offset_grad = offset_sum * grad_scale
    return (node_out, feat_grad, self_grad, neigh_grad, offset_grad)


def solution(mesh):
    return jax.shard_map(
        body,
        mesh=mesh,
        in_specs=(
            P(("row", "col"), None),
            P(("row", "col")),
            P("row", "col", None, None, None),
            P("row", "col", None),
            P("row", "col"),
            P(),
            P(),
            P(),
            P(("row", "col"), None),
        ),
        out_specs=(P(("row", "col"), None), P(("row", "col"), None), P(), P(), P()),
        check_vma=False,
    )
```

profile of v0, /device:TPU:1, one launch (start us, length us, event | category | flops | bytes accessed | tf_op | source)
XLA Modules:
  0.0 878.9 jit_solution(13381560291150448598)
XLA Ops:
  7.2 0.0 copy-start
  7.2 0.0 all-gather.3.cloned.1.call-start
  7.2 2.1 convolution_convert_fusion
  9.4 0.0 all-gather.3.cloned.1.call-update
  9.4 0.0 reduce-scatter.2.cloned.1.call-start
  10.1 0.7 fusion.12
  10.8 79.1 %all-gather.3.cloned.1.call-done = bf16[2048,256]{1,0:T(8,128)(2,1)} async-done(((bf16[128,256]{1,0:T(8,128)(2,1)}), bf16[2048,256]{1,0:T(8,128)(2,1)}) %all-gather.3.cloned.1.call-update) | async-done | bytes 1048592 | tf_op jit(solution)/shard_map/all_gather | solution.py:25
  89.9 6.7 gather_fusion
  96.6 0.0 copy-done
  96.6 7.4 convolution_bitcast_fusion.1
  104.0 9.6 %copy.19 = f32[72,128,256]{2,1,0:T(8,128)} copy(f32[72,128,256]{1,2,0:T(8,128)} %convolution_bitcast_fusion.1) | data formatting | bytes 18874368 | tf_op jit(solution)/shard_map/kij,kjh->kih/dot_general | solution.py:27
  113.6 2.6 broadcast_in_dim.9
  116.3 23.8 %scatter_fusion = f32[33,128,256]{2,1,0:T(8,128)} fusion(f32[33,128,256]{2,1,0:T(8,128)} %broadcast_in_dim.9, s32[72]{0:T(128)S(1)} %get-tuple-element.25, f32[72,128,256]{2,1,0:T(8,128)} %copy.19), kind=kCustom, calls=%fused_computation.2 | custom fusion | flops 2359296 | bytes 28311840 | tf_op jit(solution)/shard_map/scatter-add | solution.py:28
  140.1 0.0 copy-start.5
  140.1 3.9 slice.18
  144.0 0.0 reduce-scatter.2.cloned.1.call-update
  144.0 0.0 all-gather.5.cloned.1.call-start
  144.1 0.0 copy-done.6
  144.1 0.0 copy-done.7
  144.1 139.3 %reduce-scatter.2.cloned.1.call-done = bf16[128,256]{1,0:T(8,128)(2,1)} async-done(((bf16[4096,256]{1,0:T(8,128)(2,1)}), bf16[128,256]{1,0:T(8,128)(2,1)}) %reduce-scatter.2.cloned.1.call-update) | async-done | bytes 65552 | tf_op jit(solution)/shard_map/reduce_scatter | solution.py:32
  283.4 0.0 copy-done.4
  283.4 1.8 fusion.15
  285.2 0.7 divide_convert_fusion
  285.9 0.0 all-gather.5.cloned.1.call-update
  285.9 0.0 all-reduce.4.cloned.1.call-start
  286.0 92.9 %all-gather.5.cloned.1.call-done = bf16[4096,256]{1,0:T(8,128)(2,1)} async-done(((bf16[128,256]{1,0:T(8,128)(2,1)}), bf16[4096,256]{1,0:T(8,128)(2,1)}) %all-gather.5.cloned.1.call-update) | async-done | bytes 2097168 | tf_op jit(solution)/shard_map/all_gather | solution.py:46
  378.9 7.2 gather_fusion.1
  386.0 7.4 convolution_bitcast_fusion
  393.4 9.6 %copy.21 = f32[72,128,256]{2,1,0:T(8,128)} copy(f32[72,128,256]{1,2,0:T(8,128)} %convolution_bitcast_fusion) | data formatting | bytes 18874368 | tf_op jit(solution)/shard_map/kij,kih->kjh/dot_general | solution.py:48
  403.0 0.2 broadcast_in_dim.19
  403.2 14.9 %scatter_fusion.1 = f32[17,128,256]{2,1,0:T(8,128)S(1)} fusion(f32[17,128,256]{2,1,0:T(8,128)S(1)} %broadcast_in_dim.19, s32[72]{0:T(128)S(1)} %get-tuple-element.23, f32[72,128,256]{2,1,0:T(8,128)} %copy.21), kind=kCustom, calls=%fused_computation.3 | custom fusion | flops 2359296 | bytes 28311840 | tf_op jit(solution)/shard_map/scatter-add | solution.py:51
  418.2 0.0 copy-start.3
  418.2 1.1 slice.19
  419.3 0.0 all-reduce.4.cloned.1.call-update
  419.3 0.0 all-reduce.6.cloned.1.call-start
  419.4 1.3 convolution_bitcast_fusion.3
  420.7 153.1 %all-reduce.4.cloned.1.call-done = bf16[2048,256]{1,0:T(8,128)(2,1)} async-done(((bf16[2048,256]{1,0:T(8,128)(2,1)}), bf16[2048,256]{1,0:T(8,128)(2,1)}) %all-reduce.4.cloned.1.call-update) | async-done | bytes 1048592 | tf_op jit(solution)/shard_map/psum | solution.py:55
  573.9 2.1 convolution_bitcast_fusion.2
  576.0 0.0 all-reduce.6.cloned.1.call-update
  576.0 108.4 %psum.31 = f32[256]{0:T(256)S(1)} all-reduce(f32[256]{0:T(256)S(1)} %get-tuple-element.17), channel_id=1, replica_groups=mesh['row'=16,'col'=32] {'row','col'}, use_global_device_ids=true, to_apply=%region_7.8 | all-reduce | flops 256 | bytes 2048 | tf_op jit(solution)/shard_map/psum | solution.py:65
  684.4 0.6 broadcast_multiply_fusion
  685.0 1.3 fusion.7
  686.3 1.9 fusion.2
  688.2 179.6 %all-reduce.6.cloned.1.call-done = (f32[1024,256]{0,1:T(8,128)}, f32[1024,256]{0,1:T(8,128)}) async-done(((f32[1024,256]{0,1:T(8,128)}, f32[1024,256]{0,1:T(8,128)}), (f32[1024,256]{0,1:T(8,128)}, f32[1024,256]{0,1:T(8,128)})) %all-reduce.6.cloned.1.call-update) | async-done | bytes 2097168 | tf_op jit(solution)/shard_map/psum | solution.py:65
  867.8 1.3 multiply_convert_fusion.1
  869.1 1.0 copy.22
  870.1 1.3 multiply_convert_fusion
  871.4 1.0 copy.23
  (14 shorter events, 0.0 us)
Async XLA Ops:
  7.2 89.4 %copy-start = (bf16[1,1,72,128,128]{4,3,2,1,0:T(8,128)(2,1)S(1)}, bf16[1,1,72,128,128]{4,3,2,1,0:T(8,128)(2,1)}, u32[]{:S(2)}) copy-start(bf16[1,1,72,128,128]{4,3,2,1,0:T(8,128)(2,1)} %param.11) | copy-start | bytes 7077892
  7.2 82.7 %all-gather.3.cloned.1.call-start = ((), (), s32[]{:S(2)}) async-start(), calls=%async_computation.1 | async-start | bytes 1114112 | tf_op jit(solution)/shard_map/all_gather | solution.py:25
  9.4 274.0 %reduce-scatter.2.cloned.1.call-start = ((), (), s32[]{:S(2)}) async-start(), calls=%async_computation.2 | async-start | bytes 2162688 | tf_op jit(solution)/shard_map/reduce_scatter | solution.py:32
  140.1 4.0 copy-start.6
  140.1 4.0 copy-start.7
  140.1 143.4 %copy-start.2 = (bf16[128,1024]{1,0:T(8,128)(2,1)S(1)}, bf16[128,1024]{1,0:T(8,128)(2,1)}, u32[]{:S(2)}) copy-start(bf16[128,1024]{1,0:T(8,128)(2,1)} %param.9) | copy-start | bytes 786436
  140.1 143.4 %copy-start.4 = (bf16[1024,256]{1,0:T(8,128)(2,1)S(1)}, bf16[1024,256]{1,0:T(8,128)(2,1)}, u32[]{:S(2)}) copy-start(bf16[1024,256]{1,0:T(8,128)(2,1)} %param.14) | copy-start | bytes 1572868
  140.1 143.4 %copy-start.5 = (bf16[128,256]{1,0:T(8,128)(2,1)S(1)}, bf16[128,256]{1,0:T(8,128)(2,1)}, u32[]{:S(2)}) copy-start(bf16[128,256]{1,0:T(8,128)(2,1)} %param.17) | copy-start | bytes 196612
  144.0 234.8 %all-gather.5.cloned.1.call-start = ((), (), s32[]{:S(2)}) async-start(), calls=%async_computation.3 | async-start | bytes 2162688 | tf_op jit(solution)/shard_map/all_gather | solution.py:46
  285.9 287.9 %all-reduce.4.cloned.1.call-start = ((), (), s32[]{:S(2)}) async-start(), calls=%async_computation.4 | async-start | bytes 2097152 | tf_op jit(solution)/shard_map/psum | solution.py:55
  418.2 268.2 %copy-start.3 = (bf16[1024,256]{1,0:T(8,128)(2,1)S(1)}, bf16[1024,256]{1,0:T(8,128)(2,1)}, u32[]{:S(2)}) copy-start(bf16[1024,256]{1,0:T(8,128)(2,1)} %param.15) | copy-start | bytes 1572868
  419.3 448.4 %all-reduce.6.cloned.1.call-start = ((), (), s32[]{:S(2)}) async-start(), calls=%async_computation.5 | async-start | bytes 4194304 | tf_op jit(solution)/shard_map/psum | solution.py:65
  576.0 296.4 %copy-start.1 = (bf16[1,1,72,128,128]{4,3,2,1,0:T(8,128)(2,1)S(1)}, bf16[1,1,72,128,128]{4,3,2,1,0:T(8,128)(2,1)}, u32[]{:S(2)}) copy-start(bf16[1,1,72,128,128]{4,3,2,1,0:T(8,128)(2,1)} %param.11) | copy-start | bytes 7077892
Sparse Core Ops, SparseCore 0:
  10.7 79.1 all-gather.2
  144.1 139.2 reduce-scatter.1
  287.9 90.8 all-gather.4
  419.5 154.3 all-reduce.3
  578.8 288.9 all-reduce.5
where the time goes:
time: 880 us; the launch traced here: 879 us
  waiting for transfers between devices  644 us (73%)
  blocking collectives  108 us (12%)
  other arithmetic  43.3 us (5%)
  local copies, waits for them, and re-layouts  43 us (5%)
  matrix products  25.4 us (3%)
  between operations  14.6 us (2%)
    psum x1, waiting for transfers between devices, body(): lax.psum((self_term, neigh_term, offset_term), ('row', 'col'))  180 us
    psum x1, waiting for transfers between devices, body(): summed = lax.psum(returned.astype(jnp.bfloat16), 'row').astype(jnp.float32)  153 us
    reduce_scatter x1, waiting for transfers between devices, body(): lax.psum_scatter(partial_value.astype(jnp.bfloat16), 'col', scatter_dimen...  139 us
    psum x1, blocking collectives, body(): lax.psum((self_term, neigh_term, offset_term), ('row', 'col'))  108 us
    all_gather x1, waiting for transfers between devices, body(): dest_rows = lax.all_gather(dscaled, 'col', axis=0, tiled=True)  92.9 us
    all_gather x1, waiting for transfers between devices, body(): row_panel = lax.all_gather(projected, 'row', axis=0, tiled=True)  79.1 us
    scatter-add x1, other arithmetic, body(): jax.ops.segment_sum(products, dest_target, num_segments=dest_count + 1)  23.8 us
  transfers between devices with their start and end apart: 5, of which 5 were waited for; matrix products, arithmetic and copies ran while one was open for 1% of the time, Pallas kernels for 0%

commit v1 on v0

v1 whole, which is shorter than its diff:
```python
import functools
import math

import jax
import jax.numpy as jnp
from jax import lax
from jax.experimental import pallas as pl
from jax.experimental.pallas import tpu as pltpu
from jax.sharding import PartitionSpec as P

MESH = pl.DeviceIdType.MESH
BF16 = jnp.bfloat16
F32 = jnp.float32
X = 4
LANES = 128
BIG = 1 << 20


def spread_t(row):
    return jnp.broadcast_to(row, (LANES, LANES)).T


def slot_tables(group, other, used, slots):
    lane = lax.broadcasted_iota(jnp.int32, (LANES, LANES), 1)
    sub = lax.broadcasted_iota(jnp.int32, (LANES, LANES), 0)
    key = jnp.where(used > 0, group * LANES + lane[:1], BIG + lane[:1])
    key_r = jnp.broadcast_to(key, (LANES, LANES))
    key_c = spread_t(key)
    grp_r = jnp.broadcast_to(group, (LANES, LANES))
    grp_c = spread_t(group)
    used_c = spread_t(used)
    other_c = spread_t(other)
    less = jnp.where(key_r < key_c, 1, 0)
    rank = jnp.sum(less, axis=1, keepdims=True)
    same = jnp.where(grp_r == grp_c, less, 0)
    keep = jnp.minimum(jnp.sum(same, axis=1, keepdims=True), 1)
    hot = rank == lane
    order = jnp.sum(jnp.where(hot, sub, 0), axis=0, keepdims=True)
    there = jnp.sum(jnp.where(hot, other_c, 0), axis=0, keepdims=True)
    keeps = jnp.sum(jnp.where(hot, keep, 0), axis=0, keepdims=True)
    upto = jnp.sum(jnp.where(grp_c <= lane, used_c, 0), axis=0, keepdims=True)
    here = jnp.sum(jnp.where(grp_c == lane, used_c, 0), axis=0, keepdims=True)
    last = jnp.where(here > 0, upto - 1, slots)
    return [order, there, keeps, last]


def kernel(
    rows, cols, slots, scale,
    feat_ref, deg_ref, blocks_ref, coords_ref, counts_ref, ws_ref, wn_ref, off_ref, cot_ref,
    node_ref, fgrad_ref, sgrad_ref, ngrad_ref, ograd_ref,
    tiles, panel, sums, part, core_in, flow_out, flow_in, yh_out, yh_in, bands, back,
    ring_out, ring_in, line_out, line_in, own_pre, fsum,
    e1_out, e1_in, e2_out, e2_in, e3_out, e3_in, e4, egather, o1, o2, o3, o4,
    table_v, table_s, copy_sem, send_sem, recv_sem,
):
    yl_n = rows // X
    z_n = cols // 4
    half = z_n // 2
    row = lax.axis_index("row")
    col = lax.axis_index("col")
    x = lax.rem(row, X)
    yl = row // X
    z = col // 4
    yh = lax.rem(col // 2, 2)
    c = lax.rem(col, 2)
    src_n = rows
    dest_n = cols

    def at(yl_=None, x_=None, z_=None, yh_=None, c_=None):
        yl_ = yl if yl_ is None else yl_
        x_ = x if x_ is None else x_
        z_ = z if z_ is None else z_
        yh_ = yh if yh_ is None else yh_
        c_ = c if c_ is None else c_
        return (yl_ * X + x_, z_ * 4 + yh_ * 2 + c_)

    def turn(i, d, n):
        return lax.rem(i + (d % n), n)

    y_n = 2 * yl_n
    y = yh * yl_n + yl

    def at_y(y_):
        return at(yl_=lax.rem(y_, yl_n), yh_=y_ // yl_n)

    x_peers = [at(x_=turn(x, d, X)) for d in range(1, X)]
    z_peers = [at(z_=turn(z, d, z_n)) for d in range(1, z_n)]
    y_peers = [at_y(turn(y, d, y_n)) for d in range(1, y_n)]
    core_peer = at(c_=1 - c)
    peers = x_peers + z_peers + y_peers + [core_peer]

    issued = []

    def put(src, dst, device):
        i = len(issued)
        copy = pltpu.make_async_remote_copy(
            src_ref=src, dst_ref=dst, send_sem=send_sem.at[i], recv_sem=recv_sem.at[i],
            device_id=device, device_id_type=MESH,
        )
        copy.start()
        issued.append(copy)
        return copy

    def dot(a, b):
        return jnp.dot(a, b, preferred_element_type=F32)

    def dot_t(a, b):
        return lax.dot_general(a, b, (((0,), (0,)), ((), ())), preferred_element_type=F32)

    def dot_nt(a, b):
        return lax.dot_general(a, b, (((1,), (1,)), ((), ())), preferred_element_type=F32)

    load = pltpu.make_async_copy(blocks_ref, tiles, copy_sem.at[0])
    load.start()
    barrier = pltpu.get_barrier_semaphore()
    for peer in peers:
        pl.semaphore_signal(barrier, inc=1, device_id=peer, device_id_type=MESH)
    panel[x * yl_n + yl] = dot(feat_ref[...], wn_ref[...]).astype(BF16)
    pl.semaphore_wait(barrier, len(peers))

    mine = panel.at[x * yl_n + yl]
    a_line = {d: put(mine, mine, at(yl_=turn(yl, d, yl_n))) for d in range(1, yl_n)}
    right, left = at(x_=turn(x, 1, X)), at(x_=turn(x, -1, X))
    a_right, a_left = {}, {}
    for d in range(yl_n):
        if d > 0:
            a_line[d].wait_recv()
        ref = panel.at[x * yl_n + turn(yl, -d, yl_n)]
        a_right[d] = put(ref, ref, right)
        a_left[d] = put(ref, ref, left)
        if d == 0:
            table_v[...] = jnp.zeros_like(table_v)
            table_v[0:1, 0:slots] = coords_ref[...]
            code = table_v[0:1, :]
            lane = lax.broadcasted_iota(jnp.int32, (1, LANES), 1)
            used = jnp.where(lane < counts_ref[0, 0], 1, 0)
            src_bits = (src_n - 1).bit_length()
            dest = lax.shift_right_logical(code, src_bits)
            src = lax.bitwise_and(code, src_n - 1)
            dest_q = lax.bitwise_and(dest, 1) * (dest_n // 2) + lax.shift_right_logical(dest, 1)
            src_q = lax.bitwise_and(src, X - 1) * yl_n + lax.shift_right_logical(src, 2)
            lines = slot_tables(dest_q, src_q, used, slots)
            lines += slot_tables(src_q, dest_q, used, slots)
            for i, line in enumerate(lines):
                table_v[i:i + 1, :] = line
            table_copy = pltpu.make_async_copy(table_v, table_s, copy_sem.at[1])
            table_copy.start()
            own_pre[...] = dot(feat_ref[...], ws_ref[...]) + off_ref[...].astype(F32)
            sums[slots] = jnp.zeros_like(sums[slots])
    fwd = []
    for d in range(yl_n):
        a_right[d].wait_recv()
        if d % 2 == 0:
            ref = panel.at[turn(x, -1, X) * yl_n + turn(yl, -d, yl_n)]
            fwd.append(put(ref, ref, right))
        a_left[d].wait_recv()
        if d % 2 == 1:
            ref = panel.at[turn(x, 1, X) * yl_n + turn(yl, -d, yl_n)]
            fwd.append(put(ref, ref, left))
    table_copy.wait()
    load.wait()
    for copy in fwd:
        copy.wait_recv()

    def products(line, matrix, operand):
        def step(k, total):
            tile = tiles[table_s[line, k]]
            rows_in = operand[table_s[line + 1, k]]
            total = total * table_s[line + 2, k].astype(F32) + matrix(tile, rows_in)
            sums[k] = total.astype(BF16)
            return total
        lax.fori_loop(0, slots, step, jnp.zeros(sums.shape[1:], F32), unroll=4)

    products(0, dot, panel)

    reach = []
    for d in range(half, 0, -1):
        reach += [d, z_n - d] if z_n - d != d else [d]
    reach += [0]
    core_copy = {}
    for d in reach:
        zz = turn(z, d, z_n)
        for h in range(2):
            q = (1 - c) * (dest_n // 2) + zz * 2 + h
            part[q] = sums[table_s[3, q]]
        ref = part.at[pl.ds((1 - c) * (dest_n // 2) + zz * 2, 2)]
        core_copy[d] = put(ref, core_in.at[pl.ds(zz * 2, 2)], core_peer)
    def take(q, _):
        part[c * (dest_n // 2) + q] = sums[table_s[3, c * (dest_n // 2) + q]]
        return 0
    lax.fori_loop(0, dest_n // 2, take, 0)

    def own2(d, r):
        q = turn(z, d, z_n) * 2 + (yh if r == 0 else 1 - yh)
        return part[c * (dest_n // 2) + q].astype(F32) + core_in[q].astype(F32)

    z_right, z_left = at(z_=turn(z, 1, z_n)), at(z_=turn(z, -1, z_n))
    flows = [(1, 0, half), (-1, 1, half), (1, 1, half - 1), (-1, 0, half - 1)]
    flow_last = {}
    ready = set()
    slot = 0
    for step in range(half):
        for way, r, top in flows:
            d = top - step
            if d < 1:
                continue
            if (way * d) % z_n not in ready:
                core_copy[(way * d) % z_n].wait_recv()
                ready.add((way * d) % z_n)
            value = own2(way * d, r)
            if step > 0:
                copy, at_slot = flow_last[(way, r)]
                copy.wait_recv()
                value = value + flow_in[at_slot].astype(F32)
            flow_out[slot] = value.astype(BF16)
            copy = put(flow_out.at[slot], flow_in.at[slot], z_right if way == 1 else z_left)
            flow_last[(way, r)] = (copy, slot)
            slot += 1
    core_copy[0].wait_recv()

    def arrived(r):
        value = own2(0, r)
        for way in (1, -1):
            if (way, r) in flow_last:
                copy, at_slot = flow_last[(way, r)]
                copy.wait_recv()
                value = value + flow_in[at_slot].astype(F32)
        return value

    yh_out[...] = arrived(1).astype(BF16)
    yh_copy = put(yh_out, yh_in, at(yh_=1 - yh))
    mine_sum = arrived(0)
    yh_copy.wait_recv()
    aggregate = mine_sum + yh_in[...].astype(F32)

    deg = jnp.broadcast_to(deg_ref[...].astype(F32), (LANES, LANES)).T
    deg = jnp.concatenate([deg] * (aggregate.shape[1] // LANES), axis=1)
    preact = own_pre[...] + aggregate / deg
    sig = jax.nn.sigmoid(preact)
    dpre = cot_ref[...].astype(F32) * sig * (1.0 + preact * (1.0 - sig))
    dpre_b = dpre.astype(BF16)
    own_band = c * (dest_n // 2) + z * 2 + yh
    bands[own_band] = (dpre / deg).astype(BF16)

    def band(d, r):
        return bands.at[c * (dest_n // 2) + turn(z, d, z_n) * 2 + (yh if r == 0 else 1 - yh)]

    def pass_on(ref, way):
        return put(ref, ref, z_right if way == 1 else z_left)

    to_core = []
    c_yh = put(band(0, 0), band(0, 0), at(yh_=1 - yh))
    hops = {}
    for way in (1, -1):
        hops[(way, 0)] = pass_on(band(0, 0), way) if (way == 1 or half > 1) else None
    to_core.append(put(band(0, 0), band(0, 0), core_peer))
    node_ref[...] = (preact * sig).astype(BF16)

    piece = feat_ref.shape[1] // (2 * X * z_n)
    f_half = feat_ref.shape[1] // 2
    f_x = f_half // X

    def all_reduce(i, value, side):
        fsum[i] = value
        e1_out[i] = fsum[i, pl.ds((1 - c) * f_half, f_half)].astype(BF16)
        copy = put(e1_out.at[i], e1_in.at[i], core_peer)
        if side is not None:
            o1[c] = side
            o_copies = [put(o1.at[c], o1.at[c], core_peer)]
        yield
        copy.wait_recv()
        fsum[i, 0:f_half] = fsum[i, pl.ds(c * f_half, f_half)] + e1_in[i].astype(F32)
        e2_out[i] = fsum[i, 0:f_half].astype(BF16)
        copies = []
        for d in range(1, X):
            there = turn(x, d, X)
            copies.append(put(e2_out.at[i, pl.ds(there * f_x, f_x)], e2_in.at[i, d], at(x_=there)))
        if side is not None:
            for o_copy in o_copies:
                o_copy.wait_recv()
            o2[x] = jnp.sum(o1[...], axis=0)
            o_copies = [put(o2.at[x], o2.at[x], peer) for peer in x_peers]
        yield
        total = fsum[i, pl.ds(x * f_x, f_x)]
        for d in range(1, X):
            copies[d - 1].wait_recv()
            total = total + e2_in[i, d].astype(F32)
        fsum[i, 0:f_x] = total
        e3_out[i] = total.astype(BF16)
        copies = []
        for d in range(1, z_n):
            there = turn(z, d, z_n)
            copies.append(put(e3_out.at[i, pl.ds(there * piece, piece)], e3_in.at[i, d], at(z_=there)))
        if side is not None:
            for o_copy in o_copies:
                o_copy.wait_recv()
            o3[z] = jnp.sum(o2[...], axis=0)
            o_copies = [put(o3.at[z], o3.at[z], peer) for peer in z_peers]
        yield
        total = fsum[i, pl.ds(z * piece, piece)]
        for d in range(1, z_n):
            copies[d - 1].wait_recv()
            total = total + e3_in[i, d].astype(F32)
        e4[i, y] = total.astype(BF16)
        copies = [put(e4.at[i, y], e4.at[i, y], peer) for peer in y_peers]
        if side is not None:
            for o_copy in o_copies:
                o_copy.wait_recv()
            o4[y] = jnp.sum(o3[...], axis=0)
            o_copies = [put(o4.at[y], o4.at[y], peer) for peer in y_peers]
        yield
        for copy in copies:
            copy.wait_recv()
        total = e4[i, 0].astype(F32)
        for there in range(1, y_n):
            total = total + e4[i, there].astype(F32)
        start = c * f_half + x * f_x + z * piece
        egather[i, pl.ds(start, piece)] = (total * scale).astype(BF16)
        ref = egather.at[i, pl.ds(start, piece)]
        copies = [put(ref, ref, peer) for peer in z_peers]
        if side is not None:
            for o_copy in o_copies:
                o_copy.wait_recv()
            ograd_ref[...] = (jnp.sum(o4[...], axis=0) * scale)[0:1]
        yield
        for copy in copies:
            copy.wait_recv()
        ref = egather.at[i, pl.ds(c * f_half + x * f_x, f_x)]
        copies = [put(ref, ref, peer) for peer in x_peers]
        yield
        for copy in copies:
            copy.wait_recv()
        ref = egather.at[i, pl.ds(c * f_half, f_half)]
        copy = put(ref, ref, core_peer)
        yield
        copy.wait_recv()
        out = sgrad_ref if i == 0 else ngrad_ref
        out[...] = egather[i]

    side = jnp.broadcast_to(jnp.sum(dpre, axis=0, keepdims=True), o1.shape[1:])
    self_steps = all_reduce(0, dot_t(feat_ref[...], dpre_b), side)
    next(self_steps)

    c_yh.wait_recv()
    for way in (1, -1):
        hops[(way, 1)] = pass_on(band(0, 1), way) if (way == -1 or half > 1) else None
    to_core.append(put(band(0, 1), band(0, 1), core_peer))
    for dist in range(1, half + 1):
        for way, r in ((1, 0), (-1, 0), (1, 1), (-1, 1)):
            if hops.get((way, r)) is None:
                continue
            hops[(way, r)].wait_recv()
            ref = band(-way * dist, r)
            top = half if (way, r) in ((1, 0), (-1, 1)) else half - 1
            hops[(way, r)] = pass_on(ref, way) if dist < top else None
            to_core.append(put(ref, ref, core_peer))
        if dist == half // 2:
            next(self_steps)
    own_pre[...] = dpre
    for copy in to_core:
        copy.wait_recv()
    next(self_steps)

    products(4, dot_t, bands)

    def take_back(q, _):
        back[q] = sums[table_s[7, q]]
        return 0
    lax.fori_loop(0, src_n, take_back, 0)

    def back_at(dx, d):
        return turn(x, dx, X) * yl_n + turn(yl, d, yl_n)

    order = list(range(1, yl_n)) + [0]
    far = {}
    for d in order:
        way = 1 if d % 2 == 0 else -1
        far[d] = put(back.at[back_at(2, d)], ring_in.at[0, d], right if way == 1 else left)
    near = {}
    for d in order:
        for way in (1, -1):
            if (d % 2 == 0) != (way == 1):
                near[(way, d)] = put(
                    back.at[back_at(way, d)], ring_in.at[1 if way == 1 else 2, d], right if way == 1 else left
                )
    for d in order:
        way = 1 if d % 2 == 0 else -1
        far[d].wait_recv()
        ring_out[d] = (back[back_at(way, d)].astype(F32) + ring_in[0, d].astype(F32)).astype(BF16)
        near[(way, d)] = put(ring_out.at[d], ring_in.at[1 if way == 1 else 2, d], right if way == 1 else left)
    next(self_steps)
    y_copy = {}
    for d in order:
        near[(1, d)].wait_recv()
        near[(-1, d)].wait_recv()
        value = back[back_at(0, d)].astype(F32) + ring_in[1, d].astype(F32) + ring_in[2, d].astype(F32)
        if d > 0:
            line_out[d] = value.astype(BF16)
            y_copy[d] = put(line_out.at[d], line_in.at[d], at(yl_=turn(yl, d, yl_n)))
        else:
            dprop = value
    next(self_steps)
    for d in range(1, yl_n):
        y_copy[d].wait_recv()
        dprop = dprop + line_in[d].astype(F32)
    dprop_b = dprop.astype(BF16)

    neigh_steps = all_reduce(1, dot_t(feat_ref[...], dprop_b), None)
    next(neigh_steps)
    next(self_steps)
    fgrad_ref[...] = (
        dot_nt(own_pre[...].astype(BF16), ws_ref[...]) + dot_nt(dprop_b, wn_ref[...])
    ).astype(BF16)
    for step in neigh_steps:
        next(self_steps, None)
    for step in self_steps:
        pass
    for copy in issued:
        copy.wait_send()


def run(rows, cols, features, degree, blocks, coords, counts, w_self, w_neigh, offset, cotangent):
    nodes_dev, hidden = cotangent.shape
    width = features.shape[1]
    slots, side = blocks.shape[2], blocks.shape[3]
    z_n, yl_n = cols // 4, rows // X
    y_n = 2 * yl_n
    f_half = width // 2
    f_x = f_half // X
    piece = f_x // z_n
    scale = 1.0 / math.sqrt(nodes_dev * rows * cols)
    vmem = pl.BlockSpec(memory_space=pltpu.VMEM)
    block = (side, hidden)
    copies = 400
    scratch = [
        pltpu.VMEM((slots, side, side), BF16),
        pltpu.VMEM((rows,) + block, BF16),
        pltpu.VMEM((slots + 1,) + block, BF16),
        pltpu.VMEM((cols,) + block, BF16),
        pltpu.VMEM((cols // 2,) + block, BF16),
        pltpu.VMEM((2 * z_n,) + block, BF16),
        pltpu.VMEM((2 * z_n,) + block, BF16),
        pltpu.VMEM(block, BF16),
        pltpu.VMEM(block, BF16),
        pltpu.VMEM((cols,) + block, BF16),
        pltpu.VMEM((rows,) + block, BF16),
        pltpu.VMEM((yl_n,) + block, BF16),
        pltpu.VMEM((3, yl_n) + block, BF16),
        pltpu.VMEM((yl_n,) + block, BF16),
        pltpu.VMEM((yl_n,) + block, BF16),
        pltpu.VMEM((nodes_dev, hidden), F32),
        pltpu.VMEM((2, width, hidden), F32),
        pltpu.VMEM((2, f_half, hidden), BF16),
        pltpu.VMEM((2, f_half, hidden), BF16),
        pltpu.VMEM((2, f_half, hidden), BF16),
        pltpu.VMEM((2, X, f_x, hidden), BF16),
        pltpu.VMEM((2, f_x, hidden), BF16),
        pltpu.VMEM((2, z_n, piece, hidden), BF16),
        pltpu.VMEM((2, y_n, piece, hidden), BF16),
        pltpu.VMEM((2, width, hidden), BF16),
        pltpu.VMEM((2, 8, hidden), F32),
        pltpu.VMEM((X, 8, hidden), F32),
        pltpu.VMEM((z_n, 8, hidden), F32),
        pltpu.VMEM((y_n, 8, hidden), F32),
        pltpu.VMEM((8, LANES), jnp.int32),
        pltpu.SMEM((8, LANES), jnp.int32),
        pltpu.SemaphoreType.DMA((2,)),
        pltpu.SemaphoreType.DMA((copies,)),
        pltpu.SemaphoreType.DMA((copies,)),
    ]
    node_out, feat_grad, self_grad, neigh_grad, offset_grad = pl.pallas_call(
        functools.partial(kernel, rows, cols, slots, scale),
        out_shape=(
            jax.ShapeDtypeStruct((nodes_dev, hidden), BF16),
            jax.ShapeDtypeStruct((nodes_dev, width), BF16),
            jax.ShapeDtypeStruct((width, hidden), BF16),
            jax.ShapeDtypeStruct((width, hidden), BF16),
            jax.ShapeDtypeStruct((1, hidden), F32),
        ),
        in_specs=[vmem, vmem, pl.BlockSpec(memory_space=pl.ANY), vmem,
                  pl.BlockSpec(memory_space=pltpu.SMEM), vmem, vmem, vmem, vmem],
        out_specs=[vmem] * 5,
        scratch_shapes=scratch,
        compiler_params=pltpu.CompilerParams(
            collective_id=0, has_side_effects=True, vmem_limit_bytes=48 * 1024 * 1024
        ),
    )(
        features, degree.reshape(1, nodes_dev), blocks.reshape(slots, side, side),
        coords.reshape(1, slots), counts, w_self, w_neigh, offset.reshape(1, hidden), cotangent,
    )
    return node_out, feat_grad, self_grad, neigh_grad, offset_grad.reshape(hidden)


def solution(mesh):
    return jax.shard_map(
        functools.partial(run, mesh.shape["row"], mesh.shape["col"]),
        mesh=mesh,
        in_specs=(
            P(("row", "col"), None),
            P(("row", "col")),
            P("row", "col", None, None, None),
            P("row", "col", None),
            P("row", "col"),
            P(),
            P(),
            P(),
            P(("row", "col"), None),
        ),
        out_specs=(P(("row", "col"), None), P(("row", "col"), None), P(), P(), P()),
        check_vma=False,
    )
```

time: 880 us -> 148 us (0.17)
  waiting for transfers between devices: 644 us -> 0 us
  Pallas kernels: 0 us -> 136 us
  blocking collectives: 108 us -> 0 us
  other arithmetic: 43.3 us -> 0 us
  local copies, waits for them, and re-layouts: 43 us -> 11 us
  matrix products: 25.4 us -> 0 us
  between operations: 14.6 us -> 1.3 us
    psum x2 -> x0, waiting for transfers between devices: 333 us -> none  [the longest x1 180 us: body(): lax.psum((self_term, neigh_term, offset_term), ('row', 'col'))]
    all_gather x2 -> x0, waiting for transfers between devices: 172 us -> none  [the longest x1 92.9 us: body(): dest_rows = lax.all_gather(dscaled, 'col', axis=0, tiled=True)]
    reduce_scatter x1 -> x0, waiting for transfers between devices: 139 us -> none  [body(): lax.psum_scatter(partial_value.astype(jnp.bfloat16), 'col', scatter_dimen...]
    pallas_call x0 -> x1, Pallas kernels: none -> 136 us  [run(): pl.pallas_call(functools.partial(kernel, rows, cols, slots, scale), out_s...]
    psum x1 -> x0, blocking collectives: 108 us -> none  [body(): lax.psum((self_term, neigh_term, offset_term), ('row', 'col'))]
    scatter-add x2 -> x0, other arithmetic: 38.7 us -> none  [the longest x1 23.8 us: body(): jax.ops.segment_sum(products, dest_target, num_segments=dest_count + 1)]
    dot_general x8 -> x0, matrix products: 25.4 us -> none  [the longest x1 7.43 us: body(): jnp.einsum('kij,kjh->kih', tiles, picked, preferred_element_type=jnp.floa...]
    dot_general x2 -> x0, local copies, waits for them, and re-layouts: 19.2 us -> none  [the longest x1 9.63 us: body(): jnp.einsum('kij,kjh->kih', tiles, picked, preferred_element_type=jnp.floa...]
  transfers between devices with their start and end apart: 5 -> 0, of which waited for: 5 -> 0; matrix products, arithmetic and copies ran while one was open for 1% -> 0% of each run, Pallas kernels for 0% -> 0%
where the time goes in v1:
time: 148 us
  Pallas kernels  136 us (92%)
  local copies, waits for them, and re-layouts  11 us (7%)
    pallas_call x1, Pallas kernels, run(): pl.pallas_call(functools.partial(kernel, rows, cols, slots, scale), out_s...  136 us
    unnamed x19, local copies, waits for them, and re-layouts  10.3 us

profile of v1, /device:TPU:1, one launch (start us, length us, event | category | flops | bytes accessed | tf_op | source)
XLA Modules:
  0.0 148.1 jit_solution(11737937250321639556)
XLA Ops:
  1.3 0.7 reshape.28.off_ref
  1.9 0.0 copy-start
  1.9 1.7 %copy-done = bf16[1,1,72,128,128]{4,3,2,1,0:T(8,128)(2,1)S(1)} copy-done((bf16[1,1,72,128,128]{4,3,2,1,0:T(8,128)(2,1)S(1)}, bf16[1,1,72,128,128]{4,3,2,1,0:T(8,128)(2,1)}, u32[]{:S(2)}) %copy-start) | copy-done | bytes 2359320
  3.6 0.0 copy-start.1
  3.6 1.0 copy-done.1
  4.6 0.0 copy-start.2
  4.6 1.0 copy-done.2
  5.7 0.0 copy-start.3
  5.7 0.9 copy-done.3
  6.6 0.0 copy-start.4
  6.6 0.8 copy-done.4
  7.5 0.0 copy-start.5
  7.5 0.7 copy-done.5
  8.1 0.0 copy-start.6
  8.1 0.7 copy-done.6
  8.8 135.8 %shard_map.128 = (bf16[128,256]{1,0:T(8,128)(2,1)S(1)}, bf16[128,1024]{1,0:T(8,128)(2,1)S(1)}, bf16[1024,256]{1,0:T(8,128)(2,1)S(1)}, bf16[1024,256]{1,0:T(8,128)(2,1)S(1)}, f32[1,256]{1,0:T(1,128)S(1)}) custom-call(bf16[128,1024]{1,0:T(8,128)(2,1)S(1)} %copy-done.3, s32[1,128]{1,0:T(1,128)S(1)} %bitcast.6, bf16[72,128,128]{2,1,0:T(8,128)(2,1)S(1)} %bitcast.4, ...), custom_call_target="tpu_custom_call" | custom-call | tf_op jit(solution)/shard_map/pallas_call | solution.py:471
  144.6 0.6 copy.20
  145.2 0.7 copy.21
  145.9 0.8 copy.22
  146.7 0.8 copy.23
  147.5 0.6 copy.24
Async XLA Ops:
  1.9 1.7 %copy-start = (bf16[1,1,72,128,128]{4,3,2,1,0:T(8,128)(2,1)S(1)}, bf16[1,1,72,128,128]{4,3,2,1,0:T(8,128)(2,1)}, u32[]{:S(2)}) copy-start(bf16[1,1,72,128,128]{4,3,2,1,0:T(8,128)(2,1)} %param.11) | copy-start | bytes 7077892
  3.6 1.0 copy-start.1
  4.6 1.0 copy-start.2
  5.7 0.9 copy-start.3
  6.6 0.8 copy-start.4
  7.5 0.7 copy-start.5
  8.1 0.7 copy-start.6

commit v2 on v1

v2 whole, which is shorter than its diff:
```python
import functools
import math

import jax
import jax.numpy as jnp
from jax import lax
from jax.experimental import pallas as pl
from jax.experimental.pallas import tpu as pltpu
from jax.sharding import PartitionSpec as P

MESH = pl.DeviceIdType.MESH
BF16 = jnp.bfloat16
F32 = jnp.float32
X = 4
LANES = 128
BIG = 1 << 20


def spread_t(row):
    return jnp.broadcast_to(row, (LANES, LANES)).T


def slot_tables(group, other, used, slots):
    lane = lax.broadcasted_iota(jnp.int32, (LANES, LANES), 1)
    sub = lax.broadcasted_iota(jnp.int32, (LANES, LANES), 0)
    key = jnp.where(used > 0, group * LANES + lane[:1], BIG + lane[:1])
    key_r = jnp.broadcast_to(key, (LANES, LANES))
    key_c = spread_t(key)
    grp_r = jnp.broadcast_to(group, (LANES, LANES))
    grp_c = spread_t(group)
    used_c = spread_t(used)
    other_c = spread_t(other)
    less = jnp.where(key_r < key_c, 1, 0)
    rank = jnp.sum(less, axis=1, keepdims=True)
    same = jnp.where(grp_r == grp_c, less, 0)
    keep = jnp.minimum(jnp.sum(same, axis=1, keepdims=True), 1)
    hot = rank == lane
    order = jnp.sum(jnp.where(hot, sub, 0), axis=0, keepdims=True)
    there = jnp.sum(jnp.where(hot, other_c, 0), axis=0, keepdims=True)
    keeps = jnp.sum(jnp.where(hot, keep, 0), axis=0, keepdims=True)
    upto = jnp.sum(jnp.where(grp_c <= lane, used_c, 0), axis=0, keepdims=True)
    here = jnp.sum(jnp.where(grp_c == lane, used_c, 0), axis=0, keepdims=True)
    last = jnp.where(here > 0, upto - 1, slots)
    return [order, there, keeps, last]


def kernel(
    rows, cols, slots, scale,
    feat_hbm, deg_hbm, blocks_hbm, coords_hbm, counts_hbm, ws_hbm, wn_hbm, off_hbm, cot_hbm,
    node_hbm, fgrad_hbm, sgrad_hbm, ngrad_hbm, ograd_hbm,
    node_ref, fgrad_ref, ograd_ref, feats_t,
    feat_ref, deg_ref, tiles, coords_ref, counts_ref, ws_ref, wn_ref, off_ref, cot_ref,
    panel, sums, part, core_in, flow_out, flow_in, far_out, far_in, yh_out, yh_in, bands, back,
    ring_in, line_out, line_in, own_pre, fsum,
    e1_out, e1_in, e2_out, e2_in, e3_out, e3_in, e4, egather, o1, o2, o3, o4,
    table_v, table_s, copy_sem, out_sem, send_sem, recv_sem,
):
    yl_n = rows // X
    z_n = cols // 4
    row = lax.axis_index("row")
    col = lax.axis_index("col")
    x = lax.rem(row, X)
    yl = row // X
    z = col // 4
    yh = lax.rem(col // 2, 2)
    c = lax.rem(col, 2)
    src_n = rows
    dest_n = cols

    def at(yl_=None, x_=None, z_=None, yh_=None, c_=None):
        yl_ = yl if yl_ is None else yl_
        x_ = x if x_ is None else x_
        z_ = z if z_ is None else z_
        yh_ = yh if yh_ is None else yh_
        c_ = c if c_ is None else c_
        return (yl_ * X + x_, z_ * 4 + yh_ * 2 + c_)

    def turn(i, d, n):
        return lax.rem(i + (d % n), n)

    y_n = 2 * yl_n
    y = yh * yl_n + yl

    def at_y(y_):
        return at(yl_=lax.rem(y_, yl_n), yh_=y_ // yl_n)

    x_peers = [at(x_=turn(x, d, X)) for d in range(1, X)]
    z_peers = [at(z_=turn(z, d, z_n)) for d in range(1, z_n)]
    y_peers = [at_y(turn(y, d, y_n)) for d in range(1, y_n)]
    core_peer = at(c_=1 - c)
    peers = x_peers + z_peers + y_peers + [core_peer]

    near_first = sorted(range(1, yl_n), key=lambda d: min(d, yl_n - d))
    issued = []

    def put(src, dst, device):
        i = len(issued)
        copy = pltpu.make_async_remote_copy(
            src_ref=src, dst_ref=dst, send_sem=send_sem.at[i], recv_sem=recv_sem.at[i],
            device_id=device, device_id_type=MESH,
        )
        copy.start()
        issued.append(copy)
        return copy

    saved = []

    def save(src, dst):
        copy = pltpu.make_async_copy(src, dst, out_sem.at[len(saved)])
        copy.start()
        saved.append(copy)

    def dot(a, b):
        return jnp.dot(a, b, preferred_element_type=F32)

    def dot_t(a, b):
        return lax.dot_general(a, b, (((0,), (0,)), ((), ())), preferred_element_type=F32)

    def dot_nt(a, b):
        return lax.dot_general(a, b, (((1,), (1,)), ((), ())), preferred_element_type=F32)

    loads = {}
    for i, (name, there, here) in enumerate((
        ("feat", feat_hbm, feat_ref), ("wn", wn_hbm, wn_ref), ("coords", coords_hbm, coords_ref),
        ("counts", counts_hbm, counts_ref), ("ws", ws_hbm, ws_ref), ("off", off_hbm, off_ref),
        ("tiles", blocks_hbm, tiles), ("deg", deg_hbm, deg_ref), ("cot", cot_hbm, cot_ref),
    )):
        loads[name] = pltpu.make_async_copy(there, here, copy_sem.at[i])
        loads[name].start()
    barrier = pltpu.get_barrier_semaphore()
    for peer in peers:
        pl.semaphore_signal(barrier, inc=1, device_id=peer, device_id_type=MESH)
    loads["feat"].wait()
    loads["wn"].wait()
    panel[x * yl_n + yl] = dot(feat_ref[...], wn_ref[...]).astype(BF16)
    pl.semaphore_wait(barrier, len(peers))

    mine = panel.at[x * yl_n + yl]
    a_line = {d: put(mine, mine, at(yl_=turn(yl, d, yl_n))) for d in near_first}
    a_ring = [put(mine, mine, peer) for peer in x_peers]

    loads["coords"].wait()
    loads["counts"].wait()
    table_v[...] = jnp.zeros_like(table_v)
    table_v[0:1, 0:slots] = coords_ref[...]
    code = table_v[0:1, :]
    lane = lax.broadcasted_iota(jnp.int32, (1, LANES), 1)
    used = jnp.where(lane < counts_ref[0, 0], 1, 0)
    src_bits = (src_n - 1).bit_length()
    dest = lax.shift_right_logical(code, src_bits)
    src = lax.bitwise_and(code, src_n - 1)
    dest_q = lax.bitwise_and(dest, 1) * (dest_n // 2) + lax.shift_right_logical(dest, 1)
    src_q = lax.bitwise_and(src, X - 1) * yl_n + lax.shift_right_logical(src, 2)
    lines = slot_tables(dest_q, src_q, used, slots)
    lines += slot_tables(src_q, dest_q, used, slots)
    for i, line in enumerate(lines):
        table_v[i:i + 1, :] = line
    table_copy = pltpu.make_async_copy(table_v, table_s, copy_sem.at[9])
    table_copy.start()

    for d in near_first:
        a_line[d].wait_recv()
        ref = panel.at[x * yl_n + turn(yl, -d, yl_n)]
        a_ring += [put(ref, ref, peer) for peer in x_peers]
    loads["ws"].wait()
    loads["off"].wait()
    off = jnp.concatenate([off_ref[i:i + 1, :] for i in range(off_ref.shape[0])], axis=1)
    own_pre[...] = dot(feat_ref[...], ws_ref[...]) + off.astype(F32)
    sums[slots] = jnp.zeros_like(sums[slots])
    feats_t[x * yl_n + yl] = feat_ref[...].T
    loads["tiles"].wait()
    loads["deg"].wait()
    loads["cot"].wait()
    table_copy.wait()
    for copy in a_ring:
        copy.wait_recv()

    mine_t = feats_t.at[x * yl_n + yl]
    f_line = {d: put(mine_t, mine_t, at(yl_=turn(yl, d, yl_n))) for d in near_first}
    f_ring = [put(mine_t, mine_t, peer) for peer in x_peers]

    def feats_on(d):
        f_line[d].wait_recv()
        ref = feats_t.at[x * yl_n + turn(yl, -d, yl_n)]
        f_ring.extend([put(ref, ref, peer) for peer in x_peers])

    def products(line, matrix, operand):
        def step(k, total):
            tile = tiles[table_s[line, k]]
            rows_in = operand[table_s[line + 1, k]]
            total = total * table_s[line + 2, k].astype(F32) + matrix(tile, rows_in)
            sums[k] = total.astype(BF16)
            return total
        lax.fori_loop(0, slots, step, jnp.zeros(sums.shape[1:], F32), unroll=4)

    products(0, dot, panel)

    def chunk(d, r):
        return turn(z, d, z_n) * 2 + (yh if r == 0 else 1 - yh)

    core_copy = {}
    for r in (1, 0):
        for d in (4, 3, -3, 2, -2, 1, -1, 0):
            q = chunk(d, r)
            part[(1 - c) * (dest_n // 2) + q] = sums[table_s[3, (1 - c) * (dest_n // 2) + q]]
            core_copy[(d, r)] = put(part.at[(1 - c) * (dest_n // 2) + q], core_in.at[q], core_peer)

    def take(q, _):
        part[c * (dest_n // 2) + q] = sums[table_s[3, c * (dest_n // 2) + q]]
        return 0
    lax.fori_loop(0, dest_n // 2, take, 0)

    def own2(d, r):
        core_copy[(d, r)].wait_recv()
        q = chunk(d, r)
        return part[c * (dest_n // 2) + q].astype(F32) + core_in[q].astype(F32)

    def z_at(d):
        return at(z_=turn(z, d, z_n))

    mid = part.shape[1] // 2
    got = {}

    def far_dest(r):
        value = own2(4, r).astype(BF16)
        far_out[r] = value
        for i, way in enumerate((1, -1)):
            part_ref = pl.ds(i * mid, mid)
            got[(r, 4 * way)] = put(far_out.at[r, part_ref], far_in.at[r, part_ref], z_at(2 * way))
        for way in (1, -1):
            send(r, 3 * way, own2(3 * way, r), z_at(way))

    def send(r, d, value, device):
        i = r * 6 + {3: 0, -3: 1, 2: 2, -2: 3, 1: 4, -1: 5}[d]
        flow_out[i] = value.astype(BF16)
        got[(r, d)] = put(flow_out.at[i], flow_in.at[i], device)

    def came(r, d):
        got[(r, d)].wait_recv()
        return flow_in[r * 6 + {3: 0, -3: 1, 2: 2, -2: 3, 1: 4, -1: 5}[d]].astype(F32)

    def near_dest(r):
        for way in (1, -1):
            send(r, way, own2(way, r), z_at(way))

    def merged(r):
        for i, way in enumerate((1, -1)):
            value = own2(2 * way, r) + came(r, 3 * way)
            got[(r, 4 * way)].wait_recv()
            far = far_in[r, i * mid:(i + 1) * mid].astype(F32)
            if i == 0:
                value = jnp.concatenate([value[:mid] + far, value[mid:]], axis=0)
            else:
                value = jnp.concatenate([value[:mid], value[mid:] + far], axis=0)
            send(r, 2 * way, value, z_at(2 * way))

    def arrived(r):
        value = own2(0, r)
        for d in (1, -1, 2, -2):
            value = value + came(r, d)
        return value

    far_dest(1)
    near_dest(1)
    far_dest(0)
    merged(1)
    near_dest(0)
    merged(0)
    for d in near_first:
        feats_on(d)
    yh_out[...] = arrived(1).astype(BF16)
    yh_copy = put(yh_out, yh_in, at(yh_=1 - yh))
    mine_sum = arrived(0)
    yh_copy.wait_recv()
    aggregate = mine_sum + yh_in[...].astype(F32)

    deg = jnp.broadcast_to(deg_ref[...].astype(F32), (LANES, LANES)).T
    deg = jnp.concatenate([deg] * (aggregate.shape[1] // LANES), axis=1)
    preact = own_pre[...] + aggregate / deg
    sig = jax.nn.sigmoid(preact)
    dpre = cot_ref[...].astype(F32) * sig * (1.0 + preact * (1.0 - sig))
    dpre_b = dpre.astype(BF16)
    own_band = c * (dest_n // 2) + z * 2 + yh
    bands[own_band] = (dpre / deg).astype(BF16)

    def band(d, r):
        return bands.at[c * (dest_n // 2) + chunk(d, r)]

    to_core = []
    hop = {}

    def core_too(d, r):
        to_core.append(put(band(d, r), band(d, r), core_peer))

    def spread(r):
        for d in (2, -2, 1, -1):
            hop[(r, d)] = put(band(0, r), band(0, r), z_at(d))
        core_too(0, r)

    def onward(r):
        for i, way in enumerate((1, -1)):
            hop[(r, 2 * way)].wait_recv()
            ref = band(-2 * way, r)
            part_ref = ref.at[pl.ds(i * mid, mid)]
            hop[(r, 4 * way)] = put(part_ref, part_ref, z_at(2 * way))
            hop[(r, 3 * way)] = put(ref, ref, z_at(way))
            core_too(-2 * way, r)
        for way in (1, -1):
            hop[(r, way)].wait_recv()
            core_too(-way, r)

    def settle(r):
        for way in (1, -1):
            hop[(r, 3 * way)].wait_recv()
            core_too(-3 * way, r)
        for way in (1, -1):
            hop[(r, 4 * way)].wait_recv()
        core_too(4, r)

    c_yh = put(band(0, 0), band(0, 0), at(yh_=1 - yh))
    spread(0)
    node_ref[...] = (preact * sig).astype(BF16)
    save(node_ref, node_hbm)

    piece = feat_ref.shape[1] // (2 * X * z_n)
    f_half = feat_ref.shape[1] // 2
    f_x = f_half // X

    def all_reduce(i, value, side):
        if value is not None:
            fsum[i] = value
        e1_out[i] = fsum[i, pl.ds((1 - c) * f_half, f_half)].astype(BF16)
        copy = put(e1_out.at[i], e1_in.at[i], core_peer)
        if side is not None:
            o1[c] = side
            o_copies = [put(o1.at[c], o1.at[c], core_peer)]
        yield
        copy.wait_recv()
        fsum[i, 0:f_half] = fsum[i, pl.ds(c * f_half, f_half)] + e1_in[i].astype(F32)
        e2_out[i] = fsum[i, 0:f_half].astype(BF16)
        copies = []
        for d in range(1, X):
            there = turn(x, d, X)
            copies.append(put(e2_out.at[i, pl.ds(there * f_x, f_x)], e2_in.at[i, d], at(x_=there)))
        if side is not None:
            for o_copy in o_copies:
                o_copy.wait_recv()
            o2[x] = jnp.sum(o1[...], axis=0)
            o_copies = [put(o2.at[x], o2.at[x], peer) for peer in x_peers]
        yield
        total = fsum[i, pl.ds(x * f_x, f_x)]
        for d in range(1, X):
            copies[d - 1].wait_recv()
            total = total + e2_in[i, d].astype(F32)
        fsum[i, 0:f_x] = total
        e3_out[i] = total.astype(BF16)
        copies = []
        for d in range(1, z_n):
            there = turn(z, d, z_n)
            copies.append(put(e3_out.at[i, pl.ds(there * piece, piece)], e3_in.at[i, d], at(z_=there)))
        if side is not None:
            for o_copy in o_copies:
                o_copy.wait_recv()
            o3[z] = jnp.sum(o2[...], axis=0)
            o_copies = [put(o3.at[z], o3.at[z], peer) for peer in z_peers]
        yield
        total = fsum[i, pl.ds(z * piece, piece)]
        for d in range(1, z_n):
            copies[d - 1].wait_recv()
            total = total + e3_in[i, d].astype(F32)
        e4[i, y] = total.astype(BF16)
        copies = [put(e4.at[i, y], e4.at[i, y], peer) for peer in y_peers]
        if side is not None:
            for o_copy in o_copies:
                o_copy.wait_recv()
            o4[y] = jnp.sum(o3[...], axis=0)
            o_copies = [put(o4.at[y], o4.at[y], peer) for peer in y_peers]
        yield
        for copy in copies:
            copy.wait_recv()
        total = e4[i, 0].astype(F32)
        for there in range(1, y_n):
            total = total + e4[i, there].astype(F32)
        start = c * f_half + x * f_x + z * piece
        egather[i, pl.ds(start, piece)] = (total * scale).astype(BF16)
        ref = egather.at[i, pl.ds(start, piece)]
        copies = [put(ref, ref, peer) for peer in z_peers]
        if side is not None:
            for o_copy in o_copies:
                o_copy.wait_recv()
            ograd_ref[...] = (jnp.sum(o4[...], axis=0) * scale)[0:1]
            save(ograd_ref, ograd_hbm)
        yield
        for copy in copies:
            copy.wait_recv()
        ref = egather.at[i, pl.ds(c * f_half + x * f_x, f_x)]
        copies = [put(ref, ref, peer) for peer in x_peers]
        yield
        for copy in copies:
            copy.wait_recv()
        ref = egather.at[i, pl.ds(c * f_half, f_half)]
        copy = put(ref, ref, core_peer)
        yield
        copy.wait_recv()
        save(egather.at[i], sgrad_hbm if i == 0 else ngrad_hbm)

    side = jnp.broadcast_to(jnp.sum(dpre, axis=0, keepdims=True), o1.shape[1:])
    self_steps = all_reduce(0, dot(feats_t[x * yl_n + yl], dpre_b), side)
    next(self_steps)

    own_pre[...] = dpre
    onward(0)
    c_yh.wait_recv()
    spread(1)
    settle(0)
    onward(1)
    next(self_steps)
    settle(1)
    for copy in to_core:
        copy.wait_recv()

    products(4, dot_t, bands)

    def take_back(q, _):
        back[q] = sums[table_s[7, q]]
        return 0
    lax.fori_loop(0, src_n, take_back, 0)

    def back_at(dx, d):
        return turn(x, dx, X) * yl_n + turn(yl, d, yl_n)

    for copy in f_ring:
        copy.wait_recv()

    def share(m, _):
        at_m = pl.ds(pl.multiple_of(m * LANES, LANES), LANES)
        total = jnp.zeros((LANES, back.shape[2]), F32)
        for q in range(0, src_n, 2):
            left_in = jnp.concatenate([feats_t[q, at_m], feats_t[q + 1, at_m]], axis=1)
            right_in = back[q:q + 2].reshape(2 * back.shape[1], back.shape[2])
            total = total + dot(left_in, right_in)
        fsum[1, at_m] = total
        return 0
    lax.fori_loop(0, feats_t.shape[1] // LANES, share, 0)

    neigh_steps = all_reduce(1, None, None)
    next(neigh_steps)
    next(self_steps)
    next(neigh_steps)

    order = near_first[::-1] + [0]
    ring = {}
    for d in order:
        for dx in range(1, X):
            ring[(dx, d)] = put(back.at[back_at(dx, d)], ring_in.at[dx - 1, d], x_peers[dx - 1])
    next(self_steps)
    next(neigh_steps)
    next(self_steps)
    next(neigh_steps)
    y_copy = {}
    for d in order:
        value = back[back_at(0, d)].astype(F32)
        for dx in range(1, X):
            ring[(dx, d)].wait_recv()
            value = value + ring_in[dx - 1, d].astype(F32)
        if d > 0:
            line_out[d] = value.astype(BF16)
            y_copy[d] = put(line_out.at[d], line_in.at[d], at(yl_=turn(yl, d, yl_n)))
        else:
            dprop = value
    next(self_steps)
    next(neigh_steps)
    for d in range(1, yl_n):
        y_copy[d].wait_recv()
        dprop = dprop + line_in[d].astype(F32)
    fgrad_ref[...] = (
        dot_nt(own_pre[...].astype(BF16), ws_ref[...]) + dot_nt(dprop.astype(BF16), wn_ref[...])
    ).astype(BF16)
    save(fgrad_ref, fgrad_hbm)
    next(self_steps)
    next(neigh_steps)
    next(self_steps, None)
    next(neigh_steps)
    next(neigh_steps, None)
    for copy in issued:
        copy.wait_send()
    for copy in saved:
        copy.wait()


def hand_on(*refs):
    count = (len(refs) - 2) // 3
    there, here, held = refs[:count], refs[count:2 * count], refs[2 * count:3 * count]
    sem_in, sem_out = refs[-2:]
    fetch = [pltpu.make_async_copy(there[i], held[i], sem_in.at[i]) for i in range(count)]
    store = [pltpu.make_async_copy(held[i], here[i], sem_out.at[i]) for i in range(count)]
    for copy in fetch:
        copy.start()
    for i in range(count):
        fetch[i].wait()
        store[i].start()
    for copy in store:
        copy.wait()


def run(rows, cols, features, degree, blocks, coords, counts, w_self, w_neigh, offset, cotangent):
    nodes_dev, hidden = cotangent.shape
    width = features.shape[1]
    slots, side = blocks.shape[2], blocks.shape[3]
    z_n, yl_n = cols // 4, rows // X
    y_n = 2 * yl_n
    f_half = width // 2
    f_x = f_half // X
    piece = f_x // z_n
    scale = 1.0 / math.sqrt(nodes_dev * rows * cols)
    hbm = pl.BlockSpec(memory_space=pl.ANY)
    block = (side, hidden)
    copies = 400
    scratch = [
        pltpu.VMEM((nodes_dev, hidden), BF16),
        pltpu.VMEM((nodes_dev, width), BF16),
        pltpu.VMEM((1, hidden), F32),
        pltpu.VMEM((rows, width, nodes_dev), BF16),
        pltpu.VMEM((nodes_dev, width), BF16),
        pltpu.VMEM((1, nodes_dev), jnp.int32),
        pltpu.VMEM((slots, side, side), BF16),
        pltpu.VMEM((1, slots), jnp.int32),
        pltpu.SMEM((1, 1), jnp.int32),
        pltpu.VMEM((width, hidden), BF16),
        pltpu.VMEM((width, hidden), BF16),
        pltpu.VMEM((hidden // LANES, LANES), BF16),
        pltpu.VMEM((nodes_dev, hidden), BF16),
        pltpu.VMEM((rows,) + block, BF16),
        pltpu.VMEM((slots + 1,) + block, BF16),
        pltpu.VMEM((cols,) + block, BF16),
        pltpu.VMEM((cols // 2,) + block, BF16),
        pltpu.VMEM((12,) + block, BF16),
        pltpu.VMEM((12,) + block, BF16),
        pltpu.VMEM((2,) + block, BF16),
        pltpu.VMEM((2,) + block, BF16),
        pltpu.VMEM(block, BF16),
        pltpu.VMEM(block, BF16),
        pltpu.VMEM((cols,) + block, BF16),
        pltpu.VMEM((rows,) + block, BF16),
        pltpu.VMEM((3, yl_n) + block, BF16),
        pltpu.VMEM((yl_n,) + block, BF16),
        pltpu.VMEM((yl_n,) + block, BF16),
        pltpu.VMEM((nodes_dev, hidden), F32),
        pltpu.VMEM((2, width, hidden), F32),
        pltpu.VMEM((2, f_half, hidden), BF16),
        pltpu.VMEM((2, f_half, hidden), BF16),
        pltpu.VMEM((2, f_half, hidden), BF16),
        pltpu.VMEM((2, X, f_x, hidden), BF16),
        pltpu.VMEM((2, f_x, hidden), BF16),
        pltpu.VMEM((2, z_n, piece, hidden), BF16),
        pltpu.VMEM((2, y_n, piece, hidden), BF16),
        pltpu.VMEM((2, width, hidden), BF16),
        pltpu.VMEM((2, 8, hidden), F32),
        pltpu.VMEM((X, 8, hidden), F32),
        pltpu.VMEM((z_n, 8, hidden), F32),
        pltpu.VMEM((y_n, 8, hidden), F32),
        pltpu.VMEM((8, LANES), jnp.int32),
        pltpu.SMEM((8, LANES), jnp.int32),
        pltpu.SemaphoreType.DMA((10,)),
        pltpu.SemaphoreType.DMA((5,)),
        pltpu.SemaphoreType.DMA((copies,)),
        pltpu.SemaphoreType.DMA((copies,)),
    ]
    shapes = (
            jax.ShapeDtypeStruct((nodes_dev, hidden), BF16),
            jax.ShapeDtypeStruct((nodes_dev, width), BF16),
            jax.ShapeDtypeStruct((width, hidden), BF16),
            jax.ShapeDtypeStruct((width, hidden), BF16),
            jax.ShapeDtypeStruct((1, hidden), F32),
        )
    results = pl.pallas_call(
        functools.partial(kernel, rows, cols, slots, scale),
        out_shape=shapes,
        in_specs=[hbm] * 9,
        out_specs=[hbm] * 5,
        scratch_shapes=scratch,
        compiler_params=pltpu.CompilerParams(
            collective_id=0, has_side_effects=True, vmem_limit_bytes=60 * 1024 * 1024
        ),
    )(
        features, degree.reshape(1, nodes_dev), blocks.reshape(slots, side, side),
        coords.reshape(1, slots), counts, w_self, w_neigh, offset.reshape(hidden // LANES, LANES), cotangent,
    )
    node_out, feat_grad, self_grad, neigh_grad, offset_grad = pl.pallas_call(
        hand_on,
        out_shape=shapes,
        in_specs=[hbm] * 5,
        out_specs=[hbm] * 5,
        scratch_shapes=[pltpu.VMEM(held.shape, held.dtype) for held in shapes]
        + [pltpu.SemaphoreType.DMA((5,)), pltpu.SemaphoreType.DMA((5,))],
        compiler_params=pltpu.CompilerParams(vmem_limit_bytes=60 * 1024 * 1024),
    )(*results)
    return node_out, feat_grad, self_grad, neigh_grad, offset_grad.reshape(hidden)


def solution(mesh):
    return jax.shard_map(
        functools.partial(run, mesh.shape["row"], mesh.shape["col"]),
        mesh=mesh,
        in_specs=(
            P(("row", "col"), None),
            P(("row", "col")),
            P("row", "col", None, None, None),
            P("row", "col", None),
            P("row", "col"),
            P(),
            P(),
            P(),
            P(("row", "col"), None),
        ),
        out_specs=(P(("row", "col"), None), P(("row", "col"), None), P(), P(), P()),
        check_vma=False,
    )
```

time: 148 us -> 126 us (0.85)
  Pallas kernels: 136 us -> 125 us
  local copies, waits for them, and re-layouts: 11 us -> 0 us
    pallas_call x1, Pallas kernels: 136 us -> 123 us  [run(): pl.pallas_call(functools.partial(kernel, rows, cols, slots, scale), out_s...]
    unnamed x19 -> x0, local copies, waits for them, and re-layouts: 10.3 us -> none
    pallas_call x0 -> x1, Pallas kernels: none -> 2.21 us  [run(): pl.pallas_call(hand_on, out_shape=shapes, in_specs=[hbm] * 5, out_specs=[...]
where the time goes in v2:
time: 126 us
  Pallas kernels  125 us (99%)
  between operations  1.29 us (1%)
    pallas_call x1, Pallas kernels, run(): pl.pallas_call(functools.partial(kernel, rows, cols, slots, scale), out_s...  123 us

profile of v2, /device:TPU:1, one launch (start us, length us, event | category | flops | bytes accessed | tf_op | source)
XLA Modules:
  0.0 126.0 jit_solution(15974572936415469575)
XLA Ops:
  1.3 122.5 %shard_map.128 = (bf16[128,256]{1,0:T(8,128)(2,1)}, bf16[128,1024]{1,0:T(8,128)(2,1)}, bf16[1024,256]{1,0:T(8,128)(2,1)}, bf16[1024,256]{1,0:T(8,128)(2,1)}, f32[1,256]{1,0:T(1,128)}) custom-call(bf16[128,1024]{1,0:T(8,128)(2,1)} %feat_hbm.1, s32[1,128]{1,0:T(1,128)} %bitcast.6, bf16[72,128,128]{2,1,0:T(8,128)(2,1)} %bitcast.5, s32[1,72]{1,0:T(1,128)} %bitcast.7, ...), custom_call_target="tpu_custom_call" | custom-call | tf_op jit(solution)/shard_map/pallas_call | solution.py:576
  123.8 2.2 %shard_map.129 = (bf16[128,256]{1,0:T(8,128)(2,1)}, bf16[128,1024]{1,0:T(8,128)(2,1)}, bf16[1024,256]{1,0:T(8,128)(2,1)}, bf16[1024,256]{1,0:T(8,128)(2,1)}, f32[1,256]{1,0:T(1,128)}) custom-call(bf16[128,256]{1,0:T(8,128)(2,1)} %get-tuple-element.15.refs_0_, bf16[128,1024]{1,0:T(8,128)(2,1)} %get-tuple-element.16.refs_1_, ...), custom_call_target="tpu_custom_call" | custom-call | tf_op jit(solution)/shard_map/pallas_call | solution.py:589

commit v3 on v2

--- a/solution.py
+++ b/solution.py
@@ -13,7 +13,10 @@
 F32 = jnp.float32
 X = 4
 LANES = 128
+SUM_ORDER = (4, 3, -3, 1, -1, 2, -2, 0)
+HAND_ORDER = (0, 2, -2, 1, -1, 3, -3, 4)
 BIG = 1 << 20
+SEND_POOL = 48
 
 
 def spread_t(row):
@@ -48,7 +51,7 @@
     rows, cols, slots, scale,
     feat_hbm, deg_hbm, blocks_hbm, coords_hbm, counts_hbm, ws_hbm, wn_hbm, off_hbm, cot_hbm,
     node_hbm, fgrad_hbm, sgrad_hbm, ngrad_hbm, ograd_hbm,
-    node_ref, fgrad_ref, ograd_ref, feats_t,
+    node_ref, fgrad_ref, ograd_ref, feats_t, deg_t,
     feat_ref, deg_ref, tiles, coords_ref, counts_ref, ws_ref, wn_ref, off_ref, cot_ref,
     panel, sums, part, core_in, flow_out, flow_in, far_out, far_in, yh_out, yh_in, bands, back,
     ring_in, line_out, line_in, own_pre, fsum,
@@ -84,24 +87,66 @@
     def at_y(y_):
         return at(yl_=lax.rem(y_, yl_n), yh_=y_ // yl_n)
 
-    x_peers = [at(x_=turn(x, d, X)) for d in range(1, X)]
-    z_peers = [at(z_=turn(z, d, z_n)) for d in range(1, z_n)]
-    y_peers = [at_y(turn(y, d, y_n)) for d in range(1, y_n)]
+    def far_first(n):
+        return sorted(range(1, n), key=lambda d: -min(d, n - d))
+
+    x_peers = [at(x_=turn(x, d, X)) for d in far_first(X)]
+    z_peers = [at(z_=turn(z, d, z_n)) for d in far_first(z_n)]
+    y_peers = [at_y(turn(y, d, y_n)) for d in far_first(y_n)]
     core_peer = at(c_=1 - c)
-    peers = x_peers + z_peers + y_peers + [core_peer]
-
-    near_first = sorted(range(1, yl_n), key=lambda d: min(d, yl_n - d))
+    across = [at(z_=turn(z, d, z_n), yh_=1 - yh) for d in (2, -2)]
+    peers = x_peers + z_peers + y_peers + across + [core_peer]
+
+    away = range(1, yl_n)
+
+    def mate(d):
+        if d == 1:
+            return yl + 1 - 2 * lax.rem(yl, 2)
+        if d == 2:
+            return lax.rem(yl + 2, 4)
+        return 3 - yl if d == 3 else yl
+
     issued = []
+    drained = [0]
+
+    def drain(keep):
+        while drained[0] < len(issued) - keep:
+            issued[drained[0]].wait_send()
+            drained[0] += 1
+
+    def next_slot(message):
+        issued.append(message)
+        drain(SEND_POOL)
+        i = len(issued) - 1
+        return send_sem.at[i % SEND_POOL], recv_sem.at[i]
+
+    class Bundle:
+        def __init__(self, span):
+            self.span = span
+            self.send, self.recv = next_slot(self)
+
+        def put(self, src, dst, device):
+            pltpu.make_async_remote_copy(
+                src_ref=src, dst_ref=dst, send_sem=self.send, recv_sem=self.recv,
+                device_id=device, device_id_type=MESH,
+            ).start()
+
+        def wait_recv(self):
+            pltpu.make_async_copy(self.span, self.span, self.recv).wait()
+
+        def wait_send(self):
+            pltpu.make_async_copy(self.span, self.span, self.send).wait()
 
     def put(src, dst, device):
-        i = len(issued)
-        copy = pltpu.make_async_remote_copy(
-            src_ref=src, dst_ref=dst, send_sem=send_sem.at[i], recv_sem=recv_sem.at[i],
-            device_id=device, device_id_type=MESH,
-        )
-        copy.start()
-        issued.append(copy)
-        return copy
+        message = Bundle(dst)
+        message.put(src, dst, device)
+        return message
+
+    def put_all(span, ref, devices):
+        bundle = Bundle(span)
+        for device in devices:
+            bundle.put(ref, ref, device)
+        return bundle
 
     saved = []
 
@@ -136,8 +181,8 @@
     pl.semaphore_wait(barrier, len(peers))
 
     mine = panel.at[x * yl_n + yl]
-    a_line = {d: put(mine, mine, at(yl_=turn(yl, d, yl_n))) for d in near_first}
-    a_ring = [put(mine, mine, peer) for peer in x_peers]
+    a_line = {d: put(mine, mine, at(yl_=mate(d))) for d in away}
+    a_ring = put_all(panel.at[pl.ds(0, (X - 1) * yl_n)], mine, x_peers)
 
     loads["coords"].wait()
     loads["counts"].wait()
@@ -152,37 +197,45 @@
     dest_q = lax.bitwise_and(dest, 1) * (dest_n // 2) + lax.shift_right_logical(dest, 1)
     src_q = lax.bitwise_and(src, X - 1) * yl_n + lax.shift_right_logical(src, 2)
     lines = slot_tables(dest_q, src_q, used, slots)
-    lines += slot_tables(src_q, dest_q, used, slots)
+    away_z = lax.rem(lax.shift_right_logical(dest, 2) - z + z_n, z_n)
+    place = jnp.zeros_like(away_z)
+    for i, d in enumerate(HAND_ORDER):
+        place = jnp.where(away_z == d % z_n, i, place)
+    other_yh = jnp.where(lax.bitwise_and(lax.shift_right_logical(dest, 1), 1) == yh, 0, z_n)
+    hand_q = lax.bitwise_and(dest, 1) * (dest_n // 2) + other_yh + place
+    lines += slot_tables(src_q, hand_q, used, slots)
     for i, line in enumerate(lines):
         table_v[i:i + 1, :] = line
     table_copy = pltpu.make_async_copy(table_v, table_s, copy_sem.at[9])
     table_copy.start()
 
-    for d in near_first:
+    for d in away:
         a_line[d].wait_recv()
-        ref = panel.at[x * yl_n + turn(yl, -d, yl_n)]
-        a_ring += [put(ref, ref, peer) for peer in x_peers]
+        ref = panel.at[x * yl_n + mate(d)]
+        for peer in x_peers:
+            a_ring.put(ref, ref, peer)
+    feats_t[x * yl_n + yl] = feat_ref[...].T
+    mine_t = feats_t.at[x * yl_n + yl]
+    f_line = {d: put(mine_t, mine_t, at(yl_=mate(d))) for d in away}
     loads["ws"].wait()
     loads["off"].wait()
     off = jnp.concatenate([off_ref[i:i + 1, :] for i in range(off_ref.shape[0])], axis=1)
     own_pre[...] = dot(feat_ref[...], ws_ref[...]) + off.astype(F32)
     sums[slots] = jnp.zeros_like(sums[slots])
-    feats_t[x * yl_n + yl] = feat_ref[...].T
     loads["tiles"].wait()
     loads["deg"].wait()
     loads["cot"].wait()
+    deg_t[...] = spread_t(deg_ref[...].astype(F32))
     table_copy.wait()
-    for copy in a_ring:
-        copy.wait_recv()
-
-    mine_t = feats_t.at[x * yl_n + yl]
-    f_line = {d: put(mine_t, mine_t, at(yl_=turn(yl, d, yl_n))) for d in near_first}
-    f_ring = [put(mine_t, mine_t, peer) for peer in x_peers]
+    a_ring.wait_recv()
+
+    f_ring = put_all(feats_t.at[pl.ds(0, (X - 1) * yl_n)], mine_t, x_peers)
 
     def feats_on(d):
         f_line[d].wait_recv()
-        ref = feats_t.at[x * yl_n + turn(yl, -d, yl_n)]
-        f_ring.extend([put(ref, ref, peer) for peer in x_peers])
+        ref = feats_t.at[x * yl_n + mate(d)]
+        for peer in x_peers:
+            f_ring.put(ref, ref, peer)
 
     def products(line, matrix, operand):
         def step(k, total):
@@ -191,29 +244,29 @@
             total = total * table_s[line + 2, k].astype(F32) + matrix(tile, rows_in)
             sums[k] = total.astype(BF16)
             return total
-        lax.fori_loop(0, slots, step, jnp.zeros(sums.shape[1:], F32), unroll=4)
+        lax.fori_loop(0, slots, step, jnp.zeros(sums.shape[1:], F32), unroll=8)
 
     products(0, dot, panel)
 
     def chunk(d, r):
         return turn(z, d, z_n) * 2 + (yh if r == 0 else 1 - yh)
 
+    def sum_slot(d, r):
+        return (1 - r) * z_n + SUM_ORDER.index(d)
+
     core_copy = {}
     for r in (1, 0):
-        for d in (4, 3, -3, 2, -2, 1, -1, 0):
-            q = chunk(d, r)
-            part[(1 - c) * (dest_n // 2) + q] = sums[table_s[3, (1 - c) * (dest_n // 2) + q]]
-            core_copy[(d, r)] = put(part.at[(1 - c) * (dest_n // 2) + q], core_in.at[q], core_peer)
-
-    def take(q, _):
-        part[c * (dest_n // 2) + q] = sums[table_s[3, c * (dest_n // 2) + q]]
-        return 0
-    lax.fori_loop(0, dest_n // 2, take, 0)
+        for first, end in ((0, 3), (3, z_n)):
+            for d in SUM_ORDER[first:end]:
+                part[sum_slot(d, r)] = sums[table_s[3, (1 - c) * (dest_n // 2) + chunk(d, r)]]
+            span = pl.ds((1 - r) * z_n + first, end - first)
+            core_copy[(r, first)] = put(part.at[span], core_in.at[span], core_peer)
 
     def own2(d, r):
-        core_copy[(d, r)].wait_recv()
-        q = chunk(d, r)
-        return part[c * (dest_n // 2) + q].astype(F32) + core_in[q].astype(F32)
+        copy = core_copy.pop((r, 0 if d in SUM_ORDER[:3] else 3), None)
+        if copy is not None:
+            copy.wait_recv()
+        return sums[table_s[3, c * (dest_n // 2) + chunk(d, r)]].astype(F32) + core_in[sum_slot(d, r)].astype(F32)
 
     def z_at(d):
         return at(z_=turn(z, d, z_n))
@@ -252,73 +305,64 @@
                 value = jnp.concatenate([value[:mid] + far, value[mid:]], axis=0)
             else:
                 value = jnp.concatenate([value[:mid], value[mid:] + far], axis=0)
-            send(r, 2 * way, value, z_at(2 * way))
-
-    def arrived(r):
-        value = own2(0, r)
-        for d in (1, -1, 2, -2):
-            value = value + came(r, d)
-        return value
-
+            send(r, 2 * way, value, at(z_=turn(z, 2 * way, z_n), yh_=yh if r == 0 else 1 - yh))
+
+    feats_on(1)
     far_dest(1)
     near_dest(1)
     far_dest(0)
+    feats_on(2)
     merged(1)
+    feats_on(3)
+    yh_out[...] = (own2(0, 1) + came(1, 1) + came(1, -1)).astype(BF16)
+    yh_copy = put(yh_out, yh_in, at(yh_=1 - yh))
     near_dest(0)
     merged(0)
-    for d in near_first:
-        feats_on(d)
-    yh_out[...] = arrived(1).astype(BF16)
-    yh_copy = put(yh_out, yh_in, at(yh_=1 - yh))
-    mine_sum = arrived(0)
+    aggregate = own2(0, 0)
+    for r, d in ((0, 1), (0, -1), (0, 2), (0, -2), (1, 2), (1, -2)):
+        aggregate = aggregate + came(r, d)
     yh_copy.wait_recv()
-    aggregate = mine_sum + yh_in[...].astype(F32)
-
-    deg = jnp.broadcast_to(deg_ref[...].astype(F32), (LANES, LANES)).T
-    deg = jnp.concatenate([deg] * (aggregate.shape[1] // LANES), axis=1)
+    aggregate = aggregate + yh_in[...].astype(F32)
+
+    deg = jnp.concatenate([deg_t[...]] * (aggregate.shape[1] // LANES), axis=1)
     preact = own_pre[...] + aggregate / deg
     sig = jax.nn.sigmoid(preact)
     dpre = cot_ref[...].astype(F32) * sig * (1.0 + preact * (1.0 - sig))
     dpre_b = dpre.astype(BF16)
-    own_band = c * (dest_n // 2) + z * 2 + yh
-    bands[own_band] = (dpre / deg).astype(BF16)
+    bands[c * (dest_n // 2)] = (dpre / deg).astype(BF16)
 
     def band(d, r):
-        return bands.at[c * (dest_n // 2) + chunk(d, r)]
-
-    to_core = []
+        return bands.at[c * (dest_n // 2) + r * z_n + HAND_ORDER.index(d)]
+
+    to_core = Bundle(bands.at[pl.ds(0, dest_n // 2)])
     hop = {}
 
-    def core_too(d, r):
-        to_core.append(put(band(d, r), band(d, r), core_peer))
-
-    def spread(r):
-        for d in (2, -2, 1, -1):
-            hop[(r, d)] = put(band(0, r), band(0, r), z_at(d))
-        core_too(0, r)
+    def core_too(r, first, end):
+        ref = bands.at[pl.ds(c * (dest_n // 2) + r * z_n + first, end - first)]
+        to_core.put(ref, ref, core_peer)
 
     def onward(r):
         for i, way in enumerate((1, -1)):
             hop[(r, 2 * way)].wait_recv()
             ref = band(-2 * way, r)
-            part_ref = ref.at[pl.ds(i * mid, mid)]
-            hop[(r, 4 * way)] = put(part_ref, part_ref, z_at(2 * way))
-            hop[(r, 3 * way)] = put(ref, ref, z_at(way))
-            core_too(-2 * way, r)
+            rows_i = pl.ds(i * mid, mid)
+            hop[(r, 4 * way)] = put(ref.at[rows_i], band(4, r).at[rows_i], z_at(2 * way))
+            hop[(r, 3 * way)] = put(ref, band(-3 * way, r), z_at(way))
+
+    def beside(r):
         for way in (1, -1):
             hop[(r, way)].wait_recv()
-            core_too(-way, r)
+        core_too(r, 1, 5)
 
     def settle(r):
-        for way in (1, -1):
-            hop[(r, 3 * way)].wait_recv()
-            core_too(-3 * way, r)
-        for way in (1, -1):
-            hop[(r, 4 * way)].wait_recv()
-        core_too(4, r)
-
-    c_yh = put(band(0, 0), band(0, 0), at(yh_=1 - yh))
-    spread(0)
+        for d in (3, -3, 4, -4):
+            hop[(r, d)].wait_recv()
+        core_too(r, 5, z_n)
+
+    c_yh = put(band(0, 0), band(0, 1), at(yh_=1 - yh))
+    for d in (2, -2, 1, -1):
+        hop[(0, d)] = put(band(0, 0), band(-d, 0), z_at(d))
+    core_too(0, 0, 1)
     node_ref[...] = (preact * sig).astype(BF16)
     save(node_ref, node_hbm)
 
@@ -333,71 +377,64 @@
         copy = put(e1_out.at[i], e1_in.at[i], core_peer)
         if side is not None:
             o1[c] = side
-            o_copies = [put(o1.at[c], o1.at[c], core_peer)]
+            o_copy = put(o1.at[c], o1.at[c], core_peer)
         yield
         copy.wait_recv()
         fsum[i, 0:f_half] = fsum[i, pl.ds(c * f_half, f_half)] + e1_in[i].astype(F32)
         e2_out[i] = fsum[i, 0:f_half].astype(BF16)
-        copies = []
-        for d in range(1, X):
+        copies = Bundle(e2_in.at[i, pl.ds(1, X - 1)])
+        for d in far_first(X):
             there = turn(x, d, X)
-            copies.append(put(e2_out.at[i, pl.ds(there * f_x, f_x)], e2_in.at[i, d], at(x_=there)))
+            copies.put(e2_out.at[i, pl.ds(there * f_x, f_x)], e2_in.at[i, d], at(x_=there))
         if side is not None:
-            for o_copy in o_copies:
-                o_copy.wait_recv()
+            o_copy.wait_recv()
             o2[x] = jnp.sum(o1[...], axis=0)
-            o_copies = [put(o2.at[x], o2.at[x], peer) for peer in x_peers]
+            o_copy = put_all(o2.at[pl.ds(0, X - 1)], o2.at[x], x_peers)
         yield
         total = fsum[i, pl.ds(x * f_x, f_x)]
+        copies.wait_recv()
         for d in range(1, X):
-            copies[d - 1].wait_recv()
             total = total + e2_in[i, d].astype(F32)
         fsum[i, 0:f_x] = total
         e3_out[i] = total.astype(BF16)
-        copies = []
-        for d in range(1, z_n):
+        copies = Bundle(e3_in.at[i, pl.ds(1, z_n - 1)])
+        for d in far_first(z_n):
             there = turn(z, d, z_n)
-            copies.append(put(e3_out.at[i, pl.ds(there * piece, piece)], e3_in.at[i, d], at(z_=there)))
+            copies.put(e3_out.at[i, pl.ds(there * piece, piece)], e3_in.at[i, d], at(z_=there))
         if side is not None:
-            for o_copy in o_copies:
-                o_copy.wait_recv()
+            o_copy.wait_recv()
             o3[z] = jnp.sum(o2[...], axis=0)
-            o_copies = [put(o3.at[z], o3.at[z], peer) for peer in z_peers]
+            o_copy = put_all(o3.at[pl.ds(0, z_n - 1)], o3.at[z], z_peers)
         yield
         total = fsum[i, pl.ds(z * piece, piece)]
+        copies.wait_recv()
         for d in range(1, z_n):
-            copies[d - 1].wait_recv()
             total = total + e3_in[i, d].astype(F32)
         e4[i, y] = total.astype(BF16)
-        copies = [put(e4.at[i, y], e4.at[i, y], peer) for peer in y_peers]
+        copies = put_all(e4.at[i, pl.ds(0, y_n - 1)], e4.at[i, y], y_peers)
         if side is not None:
-            for o_copy in o_copies:
-                o_copy.wait_recv()
+            o_copy.wait_recv()
             o4[y] = jnp.sum(o3[...], axis=0)
-            o_copies = [put(o4.at[y], o4.at[y], peer) for peer in y_peers]
+            o_copy = put_all(o4.at[pl.ds(0, y_n - 1)], o4.at[y], y_peers)
         yield
-        for copy in copies:
-            copy.wait_recv()
+        copies.wait_recv()
         total = e4[i, 0].astype(F32)
         for there in range(1, y_n):
             total = total + e4[i, there].astype(F32)
         start = c * f_half + x * f_x + z * piece
         egather[i, pl.ds(start, piece)] = (total * scale).astype(BF16)
         ref = egather.at[i, pl.ds(start, piece)]
-        copies = [put(ref, ref, peer) for peer in z_peers]
+        copies = put_all(egather.at[i, pl.ds(0, (z_n - 1) * piece)], ref, z_peers)
         if side is not None:
-            for o_copy in o_copies:
-                o_copy.wait_recv()
+            o_copy.wait_recv()
             ograd_ref[...] = (jnp.sum(o4[...], axis=0) * scale)[0:1]
             save(ograd_ref, ograd_hbm)
         yield
-        for copy in copies:
-            copy.wait_recv()
+        copies.wait_recv()
         ref = egather.at[i, pl.ds(c * f_half + x * f_x, f_x)]
-        copies = [put(ref, ref, peer) for peer in x_peers]
+        copies = put_all(egather.at[i, pl.ds(0, (X - 1) * f_x)], ref, x_peers)
         yield
-        for copy in copies:
-            copy.wait_recv()
+        copies.wait_recv()
         ref = egather.at[i, pl.ds(c * f_half, f_half)]
         copy = put(ref, ref, core_peer)
         yield
@@ -409,15 +446,20 @@
     next(self_steps)
 
     own_pre[...] = dpre
+    c_yh.wait_recv()
+    for d in (2, -2):
+        hop[(1, d)] = put(band(0, 1), band(-d, 1), z_at(d))
     onward(0)
-    c_yh.wait_recv()
-    spread(1)
+    for d in (1, -1):
+        hop[(1, d)] = put(band(0, 1), band(-d, 1), z_at(d))
+    core_too(1, 0, 1)
+    beside(0)
+    onward(1)
     settle(0)
-    onward(1)
     next(self_steps)
+    beside(1)
     settle(1)
-    for copy in to_core:
-        copy.wait_recv()
+    to_core.wait_recv()
 
     products(4, dot_t, bands)
 
@@ -427,10 +469,9 @@
     lax.fori_loop(0, src_n, take_back, 0)
 
     def back_at(dx, d):
-        return turn(x, dx, X) * yl_n + turn(yl, d, yl_n)
-
-    for copy in f_ring:
-        copy.wait_recv()
+        return turn(x, dx, X) * yl_n + mate(d)
+
+    f_ring.wait_recv()
 
     def share(m, _):
         at_m = pl.ds(pl.multiple_of(m * LANES, LANES), LANES)
@@ -441,20 +482,23 @@
             total = total + dot(left_in, right_in)
         fsum[1, at_m] = total
         return 0
-    lax.fori_loop(0, feats_t.shape[1] // LANES, share, 0)
-
+    f_tiles = f_half // LANES
+    lax.fori_loop((1 - c) * f_tiles, (2 - c) * f_tiles, share, 0)
     neigh_steps = all_reduce(1, None, None)
     next(neigh_steps)
+    lax.fori_loop(c * f_tiles, (1 + c) * f_tiles, share, 0)
+    drain(12)
     next(self_steps)
     next(neigh_steps)
 
-    order = near_first[::-1] + [0]
+    order = [3, 2, 1, 0]
     ring = {}
     for d in order:
-        for dx in range(1, X):
-            ring[(dx, d)] = put(back.at[back_at(dx, d)], ring_in.at[dx - 1, d], x_peers[dx - 1])
+        for dx in far_first(X):
+            ring[(dx, d)] = put(back.at[back_at(dx, d)], ring_in.at[dx - 1, d], at(x_=turn(x, dx, X)))
     next(self_steps)
     next(neigh_steps)
+    drain(24)
     next(self_steps)
     next(neigh_steps)
     y_copy = {}
@@ -465,11 +509,12 @@
             value = value + ring_in[dx - 1, d].astype(F32)
         if d > 0:
             line_out[d] = value.astype(BF16)
-            y_copy[d] = put(line_out.at[d], line_in.at[d], at(yl_=turn(yl, d, yl_n)))
+            y_copy[d] = put(line_out.at[d], line_in.at[d], at(yl_=mate(d)))
         else:
             dprop = value
     next(self_steps)
     next(neigh_steps)
+    drain(8)
     for d in range(1, yl_n):
         y_copy[d].wait_recv()
         dprop = dprop + line_in[d].astype(F32)
@@ -480,10 +525,11 @@
     next(self_steps)
     next(neigh_steps)
     next(self_steps, None)
+    drain(3)
     next(neigh_steps)
+    drain(1)
     next(neigh_steps, None)
-    for copy in issued:
-        copy.wait_send()
+    drain(0)
     for copy in saved:
         copy.wait()
 
@@ -515,12 +561,13 @@
     scale = 1.0 / math.sqrt(nodes_dev * rows * cols)
     hbm = pl.BlockSpec(memory_space=pl.ANY)
     block = (side, hidden)
-    copies = 400
+    copies = 80
     scratch = [
         pltpu.VMEM((nodes_dev, hidden), BF16),
         pltpu.VMEM((nodes_dev, width), BF16),
         pltpu.VMEM((1, hidden), F32),
         pltpu.VMEM((rows, width, nodes_dev), BF16),
+        pltpu.VMEM((LANES, LANES), F32),
         pltpu.VMEM((nodes_dev, width), BF16),
         pltpu.VMEM((1, nodes_dev), jnp.int32),
         pltpu.VMEM((slots, side, side), BF16),
@@ -532,7 +579,7 @@
         pltpu.VMEM((nodes_dev, hidden), BF16),
         pltpu.VMEM((rows,) + block, BF16),
         pltpu.VMEM((slots + 1,) + block, BF16),
-        pltpu.VMEM((cols,) + block, BF16),
+        pltpu.VMEM((cols // 2,) + block, BF16),
         pltpu.VMEM((cols // 2,) + block, BF16),
         pltpu.VMEM((12,) + block, BF16),
         pltpu.VMEM((12,) + block, BF16),
@@ -563,7 +610,7 @@
         pltpu.SMEM((8, LANES), jnp.int32),
         pltpu.SemaphoreType.DMA((10,)),
         pltpu.SemaphoreType.DMA((5,)),
-        pltpu.SemaphoreType.DMA((copies,)),
+        pltpu.SemaphoreType.DMA((SEND_POOL,)),
         pltpu.SemaphoreType.DMA((copies,)),
     ]
     shapes = (

time: 126 us -> 116 us (0.921)
  Pallas kernels: 125 us -> 115 us
    pallas_call x1, Pallas kernels: 123 us -> 113 us  [run(): pl.pallas_call(functools.partial(kernel, rows, cols, slots, scale), out_s...]
where the time goes in v3:
time: 116 us
  Pallas kernels  115 us (99%)
  between operations  1.29 us (1%)
    pallas_call x1, Pallas kernels, run(): pl.pallas_call(functools.partial(kernel, rows, cols, slots, scale), out_s...  113 us

profile of v3, /device:TPU:1, one launch (start us, length us, event | category | flops | bytes accessed | tf_op | source)
XLA Modules:
  0.0 116.2 jit_solution(11318026692935877432)
XLA Ops:
  1.3 112.7 %shard_map.128 = (bf16[128,256]{1,0:T(8,128)(2,1)}, bf16[128,1024]{1,0:T(8,128)(2,1)}, bf16[1024,256]{1,0:T(8,128)(2,1)}, bf16[1024,256]{1,0:T(8,128)(2,1)}, f32[1,256]{1,0:T(1,128)}) custom-call(bf16[128,1024]{1,0:T(8,128)(2,1)} %feat_hbm.1, s32[1,128]{1,0:T(1,128)} %bitcast.6, bf16[72,128,128]{2,1,0:T(8,128)(2,1)} %bitcast.5, s32[1,72]{1,0:T(1,128)} %bitcast.7, ...), custom_call_target="tpu_custom_call" | custom-call | tf_op jit(solution)/shard_map/pallas_call | solution.py:623
  114.0 2.2 %shard_map.129 = (bf16[128,256]{1,0:T(8,128)(2,1)}, bf16[128,1024]{1,0:T(8,128)(2,1)}, bf16[1024,256]{1,0:T(8,128)(2,1)}, bf16[1024,256]{1,0:T(8,128)(2,1)}, f32[1,256]{1,0:T(1,128)}) custom-call(bf16[128,256]{1,0:T(8,128)(2,1)} %get-tuple-element.15.refs_0_, bf16[128,1024]{1,0:T(8,128)(2,1)} %get-tuple-element.16.refs_1_, ...), custom_call_target="tpu_custom_call" | custom-call | tf_op jit(solution)/shard_map/pallas_call | solution.py:636

commit v4 on v3

--- a/solution.py
+++ b/solution.py
@@ -94,8 +94,7 @@
     z_peers = [at(z_=turn(z, d, z_n)) for d in far_first(z_n)]
     y_peers = [at_y(turn(y, d, y_n)) for d in far_first(y_n)]
     core_peer = at(c_=1 - c)
-    across = [at(z_=turn(z, d, z_n), yh_=1 - yh) for d in (2, -2)]
-    peers = x_peers + z_peers + y_peers + across + [core_peer]
+    peers = z_peers + y_peers + x_peers + [core_peer]
 
     away = range(1, yl_n)
 
@@ -164,6 +163,9 @@
     def dot_nt(a, b):
         return lax.dot_general(a, b, (((1,), (1,)), ((), ())), preferred_element_type=F32)
 
+    barrier = pltpu.get_barrier_semaphore()
+    for peer in peers:
+        pl.semaphore_signal(barrier, inc=1, device_id=peer, device_id_type=MESH)
     loads = {}
     for i, (name, there, here) in enumerate((
         ("feat", feat_hbm, feat_ref), ("wn", wn_hbm, wn_ref), ("coords", coords_hbm, coords_ref),
@@ -172,9 +174,6 @@
     )):
         loads[name] = pltpu.make_async_copy(there, here, copy_sem.at[i])
         loads[name].start()
-    barrier = pltpu.get_barrier_semaphore()
-    for peer in peers:
-        pl.semaphore_signal(barrier, inc=1, device_id=peer, device_id_type=MESH)
     loads["feat"].wait()
     loads["wn"].wait()
     panel[x * yl_n + yl] = dot(feat_ref[...], wn_ref[...]).astype(BF16)
@@ -305,7 +304,7 @@
                 value = jnp.concatenate([value[:mid] + far, value[mid:]], axis=0)
             else:
                 value = jnp.concatenate([value[:mid], value[mid:] + far], axis=0)
-            send(r, 2 * way, value, at(z_=turn(z, 2 * way, z_n), yh_=yh if r == 0 else 1 - yh))
+            send(r, 2 * way, value, z_at(2 * way))
 
     feats_on(1)
     far_dest(1)
@@ -314,13 +313,16 @@
     feats_on(2)
     merged(1)
     feats_on(3)
-    yh_out[...] = (own2(0, 1) + came(1, 1) + came(1, -1)).astype(BF16)
-    yh_copy = put(yh_out, yh_in, at(yh_=1 - yh))
     near_dest(0)
     merged(0)
+    others = own2(0, 1)
+    for d in (1, -1, 2, -2):
+        others = others + came(1, d)
+    yh_out[...] = others.astype(BF16)
+    yh_copy = put(yh_out, yh_in, at(yh_=1 - yh))
     aggregate = own2(0, 0)
-    for r, d in ((0, 1), (0, -1), (0, 2), (0, -2), (1, 2), (1, -2)):
-        aggregate = aggregate + came(r, d)
+    for d in (1, -1, 2, -2):
+        aggregate = aggregate + came(0, d)
     yh_copy.wait_recv()
     aggregate = aggregate + yh_in[...].astype(F32)
 

time: 116 us -> 112 us (0.966)
  Pallas kernels: 115 us -> 110 us
    pallas_call x1, Pallas kernels: 113 us -> 108 us  [run(): pl.pallas_call(functools.partial(kernel, rows, cols, slots, scale), out_s...]
where the time goes in v4:
time: 112 us; the launch traced here: 111 us
  Pallas kernels  110 us (98%)
  between operations  1.29 us (1%)
    pallas_call x1, Pallas kernels, run(): pl.pallas_call(functools.partial(kernel, rows, cols, slots, scale), out_s...  108 us

profile of v4, /device:TPU:1, one launch (start us, length us, event | category | flops | bytes accessed | tf_op | source)
XLA Modules:
  0.0 111.4 jit_solution(3441865390335559572)
XLA Ops:
  1.3 107.9 %shard_map.128 = (bf16[128,256]{1,0:T(8,128)(2,1)}, bf16[128,1024]{1,0:T(8,128)(2,1)}, bf16[1024,256]{1,0:T(8,128)(2,1)}, bf16[1024,256]{1,0:T(8,128)(2,1)}, f32[1,256]{1,0:T(1,128)}) custom-call(bf16[128,1024]{1,0:T(8,128)(2,1)} %feat_hbm.1, s32[1,128]{1,0:T(1,128)} %bitcast.6, bf16[72,128,128]{2,1,0:T(8,128)(2,1)} %bitcast.5, s32[1,72]{1,0:T(1,128)} %bitcast.7, ...), custom_call_target="tpu_custom_call" | custom-call | tf_op jit(solution)/shard_map/pallas_call | solution.py:625
  109.2 2.2 %shard_map.129 = (bf16[128,256]{1,0:T(8,128)(2,1)}, bf16[128,1024]{1,0:T(8,128)(2,1)}, bf16[1024,256]{1,0:T(8,128)(2,1)}, bf16[1024,256]{1,0:T(8,128)(2,1)}, f32[1,256]{1,0:T(1,128)}) custom-call(bf16[128,256]{1,0:T(8,128)(2,1)} %get-tuple-element.15.refs_0_, bf16[128,1024]{1,0:T(8,128)(2,1)} %get-tuple-element.16.refs_1_, ...), custom_call_target="tpu_custom_call" | custom-call | tf_op jit(solution)/shard_map/pallas_call | solution.py:638
